TPU v7x, 32 devices: a whole 2x2x4 slice. The times are simulated.
32 devices in a mesh: roi: 16 (over z, y, core), ch: 2 (over x).
Axes of the slice: x: 2, y: 2, z: 4, core: 2. Of those that a mesh axis runs over, the one named last changes fastest.
Arguments:
- pyramid_two: bfloat16 [32, 256, 4096], P('roi', 'ch'), may hold values from -6 to 6
- pyramid_three: bfloat16 [32, 256, 1024], P('roi', 'ch'), may hold values from -6 to 6
- pyramid_four: bfloat16 [32, 256, 256], P('roi', 'ch'), may hold values from -6 to 6
- pyramid_five: bfloat16 [32, 256, 64], P('roi', 'ch'), may hold values from -6 to 6
- proposals: float32 [4, 8192], P(None, 'roi'), may hold values from 0 to 1, as said below
- image_index: int32 [8192], P('roi'), may hold values from 0 to 31, as said below
- levels: int32 [8192], P('roi'), may hold values from 0 to 3
- labels: int32 [8192], P('roi'), may hold values from 0 to 80
- targets: float32 [4, 8192], P(None, 'roi'), may hold values from -6 to 6
- first_weight: bfloat16 [12544, 1024], P('ch'), may hold values from -0.0546875 to 0.0546875
- first_bias: bfloat16 [1024], replicated, may hold values from -3 to 3
- second_weight: bfloat16 [1024, 1024], replicated, may hold values from -0.1875 to 0.1875
- second_bias: bfloat16 [1024], replicated, may hold values from -3 to 3
- class_weight: bfloat16 [1024, 81], replicated, may hold values from -0.75 to 0.75
- class_bias: bfloat16 [81], replicated, may hold values from -4 to 4
- box_weight: bfloat16 [1024, 4], replicated, may hold values from -0.375 to 0.375
- box_bias: bfloat16 [4], replicated, may hold values from -3 to 3
Outputs:
- class_loss: float32 [], replicated
- box_loss: float32 [], replicated
- decoded: float32 [4, 8192], P(None, ('roi', 'ch'))
- first_weight_grad: float32 [12544, 1024], P('ch')
- first_bias_grad: float32 [1024], replicated
- second_weight_grad: float32 [1024, 1024], replicated
- second_bias_grad: float32 [1024], replicated
- class_weight_grad: float32 [1024, 81], replicated
- class_bias_grad: float32 [81], replicated
- box_weight_grad: float32 [1024, 4], replicated
- box_bias_grad: float32 [4], replicated
- pyramid_two_grad: float32 [32, 256, 4096], P('roi', 'ch')
- pyramid_three_grad: float32 [32, 256, 1024], P('roi', 'ch')
- pyramid_four_grad: float32 [32, 256, 256], P('roi', 'ch')
- pyramid_five_grad: float32 [32, 256, 64], P('roi', 'ch')
Inputs may be any that keep to these rules, and one draw needn't show every extreme that they name: `proposals`: x1 < x2 and y1 < y2; every box is 1/64 of the image side wide and high or more. `image_index`: region r lies in one of the images 2 * (r // 512) to 2 * (r // 512) + 1; earlier images of such a group hold more regions.
All inputs are finite; a program needn't handle non-finite values.
Results may differ from a plain program's by a relative error of at most 0.0095.
Values may be sent and summed in bfloat16 or wider, within the bound.
No kernel may reach another device: no remote copies, remote signals or barrier semaphores. Data moves between devices by JAX's collectives and lax.ppermute only.
A program may use at most 256 MiB of HBM per device.

v0:
```python
import jax
import jax.numpy as jnp
from jax import lax
from jax.sharding import PartitionSpec as P

POOL = 7
SAMPLES = 2
SIDE = 64
BLOCK = 128


def smooth_unit(values):
    return jax.nn.gelu(values, approximate=False)


def spread_weights(low_edge, high_edge, extent):
    anchor = low_edge * extent - 0.5
    stride = (high_edge - low_edge) * extent / POOL
    columns = jnp.arange(POOL, dtype=jnp.float32)
    places = jnp.arange(extent, dtype=jnp.float32)
    weights = jnp.zeros((low_edge.shape[0], POOL, extent), jnp.float32)
    for sample in range(SAMPLES):
        located = anchor[:, None] + (columns[None, :] + (sample + 0.5) / SAMPLES) * stride[:, None]
        located = jnp.clip(located, 0.0, extent - 1.0)
        weights = weights + jnp.maximum(
            0.0, 1.0 - jnp.abs(located[:, :, None] - places[None, None, :])
        )
    return weights / SAMPLES


def level_tables(corners, local_image, level_ids, level_num, images_here):
    extent = SIDE // 2**level_num
    across = spread_weights(corners[0], corners[2], extent)
    downward = spread_weights(corners[1], corners[3], extent)
    picked = (local_image[:, None] == jnp.arange(images_here, dtype=jnp.int32)[None, :]) & (
        level_ids[:, None] == level_num
    )
    select = picked.astype(jnp.float32)[:, :, None, None] * across[:, None, :, :]
    select = jnp.transpose(select, (1, 3, 0, 2)).reshape(images_here * extent, -1)
    return (select.astype(jnp.bfloat16), downward)


def as_matrix(feature, level_num):
    extent = SIDE // 2**level_num
    images_here, channels_here = (feature.shape[0], feature.shape[1])
    shaped = feature.reshape(images_here, channels_here, extent, extent).transpose(1, 2, 0, 3)
    return shaped.reshape(channels_here * extent, images_here * extent)


def pool_forward(matrices, corners, local_image, level_ids, channels_here, images_here):
    region_count = corners.shape[1]
    pooled_sum = jnp.zeros((region_count, channels_here, POOL, POOL), jnp.float32)
    for level_num in range(4):
        extent = SIDE // 2**level_num
        select, downward = level_tables(corners, local_image, level_ids, level_num, images_here)
        section_one = jnp.dot(matrices[level_num], select, preferred_element_type=jnp.float32)
        section_one = section_one.reshape(channels_here, extent, region_count, POOL)
        pooled_sum = pooled_sum + jnp.einsum(
            "rih,chrj->rcij", downward, section_one, precision=lax.Precision.HIGHEST
        )
    return pooled_sum.reshape(region_count, -1).astype(jnp.bfloat16)


def pool_backward(running, pieces, channels_here, images_here):
    corners, local_image, level_ids, grad_rows = pieces
    region_count = corners.shape[1]
    grad_cells = grad_rows.astype(jnp.float32).reshape(region_count, channels_here, POOL, POOL)
    updated = []
    for level_num in range(4):
        extent = SIDE // 2**level_num
        select, downward = level_tables(corners, local_image, level_ids, level_num, images_here)
        grad_section = jnp.einsum(
            "rih,rcij->chrj", downward, grad_cells, precision=lax.Precision.HIGHEST
        )
        grad_section = grad_section.astype(jnp.bfloat16).reshape(
            channels_here * extent, region_count * POOL
        )
        updated.append(
            running[level_num]
            + lax.dot_general(
                grad_section, select, (((1,), (1,)), ((), ())), preferred_element_type=jnp.float32
            )
        )
    return tuple(updated)


def decode_boxes(corners, deltas):
    widths = corners[2] - corners[0]
    heights = corners[3] - corners[1]
    centre_x = corners[0] + 0.5 * widths
    centre_y = corners[1] + 0.5 * heights
    moved_x = deltas[:, 0] / 10.0 * widths + centre_x
    moved_y = deltas[:, 1] / 10.0 * heights + centre_y
    new_width = jnp.exp(deltas[:, 2] / 5.0) * widths
    new_height = jnp.exp(deltas[:, 3] / 5.0) * heights
    return jnp.stack(
        [
            moved_x - 0.5 * new_width,
            moved_y - 0.5 * new_height,
            moved_x + 0.5 * new_width,
            moved_y + 0.5 * new_height,
        ]
    )


def column_sums(matrix):
    return jnp.sum(matrix.astype(jnp.float32), axis=0)


def transposed_product(left_rows, right_rows):
    return lax.dot_general(
        left_rows, right_rows, (((0,), (0,)), ((), ())), preferred_element_type=jnp.float32
    )


def product_with_transpose(left_rows, right_rows):
    return lax.dot_general(
        left_rows, right_rows, (((1,), (1,)), ((), ())), preferred_element_type=jnp.float32
    )


def head_pass(
    summed,
    first_bias,
    second_weight,
    second_bias,
    class_weight,
    class_bias,
    box_weight,
    box_bias,
    label_rows,
    target_rows,
    corner_rows,
    norm_count,
):
    pre_one = summed + first_bias.astype(jnp.float32)
    act_one, gelu_one = jax.vjp(smooth_unit, pre_one)
    act_one = act_one.astype(jnp.bfloat16)
    pre_two = jnp.dot(
        act_one, second_weight, preferred_element_type=jnp.float32
    ) + second_bias.astype(jnp.float32)
    act_two, gelu_two = jax.vjp(smooth_unit, pre_two)
    act_two = act_two.astype(jnp.bfloat16)
    logits = jnp.dot(act_two, class_weight, preferred_element_type=jnp.float32) + class_bias.astype(
        jnp.float32
    )
    deltas = jnp.dot(act_two, box_weight, preferred_element_type=jnp.float32) + box_bias.astype(
        jnp.float32
    )
    classes = logits.shape[1]
    row_max = jnp.max(logits, axis=1, keepdims=True)
    exponent = jnp.exp(logits - row_max)
    row_total = jnp.sum(exponent, axis=1, keepdims=True)
    onehot = (label_rows[:, None] == jnp.arange(classes, dtype=jnp.int32)[None, :]).astype(
        jnp.float32
    )
    class_part = (
        jnp.sum(row_max[:, 0] + jnp.log(row_total[:, 0]) - jnp.sum(logits * onehot, axis=1))
        / norm_count
    )
    foreground = (label_rows < classes - 1).astype(jnp.float32)[:, None]
    residue = deltas - target_rows.T
    magnitude = jnp.abs(residue)
    huber = jnp.where(magnitude < 1.0, 0.5 * residue * residue, magnitude - 0.5)
    box_part = jnp.sum(foreground * huber) / norm_count
    grad_logits = ((exponent / row_total - onehot) / norm_count).astype(jnp.bfloat16)
    grad_deltas = (foreground * jnp.clip(residue, -1.0, 1.0) / norm_count).astype(jnp.bfloat16)
    grad_weight_class = transposed_product(act_two, grad_logits)
    grad_bias_class = column_sums(grad_logits)
    grad_weight_box = transposed_product(act_two, grad_deltas)
    grad_bias_box = column_sums(grad_deltas)
    grad_act_two = product_with_transpose(grad_logits, class_weight) + product_with_transpose(
        grad_deltas, box_weight
    )
    grad_pre_two = gelu_two(grad_act_two)[0].astype(jnp.bfloat16)
    grad_weight_two = transposed_product(act_one, grad_pre_two)
    grad_bias_two = column_sums(grad_pre_two)
    grad_act_one = product_with_transpose(grad_pre_two, second_weight)
    grad_pre_one = gelu_one(grad_act_one)[0].astype(jnp.bfloat16)
    grad_bias_one = column_sums(grad_pre_one)
    decoded = decode_boxes(corner_rows, deltas)
    small_grads = (
        grad_bias_one,
        grad_weight_two,
        grad_bias_two,
        grad_weight_class,
        grad_bias_class,
        grad_weight_box,
        grad_bias_box,
        class_part,
        box_part,
    )
    return (grad_pre_one, small_grads, decoded)


def on_device(
    pyramid_two,
    pyramid_three,
    pyramid_four,
    pyramid_five,
    proposals,
    image_index,
    levels,
    labels,
    targets,
    first_weight,
    first_bias,
    second_weight,
    second_bias,
    class_weight,
    class_bias,
    box_weight,
    box_bias,
):
    features = (pyramid_two, pyramid_three, pyramid_four, pyramid_five)
    images_here, channels_here = (pyramid_two.shape[0], pyramid_two.shape[1])
    regions_here = proposals.shape[1]
    blocks = regions_here // BLOCK
    local_image = image_index - lax.axis_index("roi") * images_here
    matrices = [as_matrix(features[level_num], level_num) for level_num in range(4)]
    corner_blocks = proposals.reshape(4, blocks, BLOCK).transpose(1, 0, 2)
    image_blocks = local_image.reshape(blocks, BLOCK)
    level_blocks = levels.reshape(blocks, BLOCK)

    def forward_block(pieces):
        return pool_forward(matrices, pieces[0], pieces[1], pieces[2], channels_here, images_here)

    pooled = lax.map(forward_block, (corner_blocks, image_blocks, level_blocks)).reshape(
        regions_here, -1
    )
    norm_count = float(regions_here * lax.axis_size("roi"))
    share_rows = regions_here // lax.axis_size("ch")
    start_row = lax.axis_index("ch") * share_rows
    summed = lax.psum(jnp.dot(pooled, first_weight, preferred_element_type=jnp.float32), "ch")
    grad_pre_one, small_grads, decoded = head_pass(
        summed,
        first_bias,
        second_weight,
        second_bias,
        class_weight,
        class_bias,
        box_weight,
        box_bias,
        labels,
        targets,
        proposals,
        norm_count,
    )
    grad_weight_one = transposed_product(pooled, grad_pre_one)
    grad_pooled = product_with_transpose(grad_pre_one, first_weight).astype(jnp.bfloat16)
    (
        grad_bias_one,
        grad_weight_two,
        grad_bias_two,
        grad_weight_class,
        grad_bias_class,
        grad_weight_box,
        grad_bias_box,
        class_part,
        box_part,
    ) = small_grads
    (
        grad_weight_one,
        grad_bias_one,
        grad_weight_two,
        grad_bias_two,
        grad_weight_class,
        grad_bias_class,
        grad_weight_box,
        grad_bias_box,
        class_loss,
        box_loss,
    ) = lax.psum(
        (
            grad_weight_one,
            grad_bias_one,
            grad_weight_two,
            grad_bias_two,
            grad_weight_class,
            grad_bias_class,
            grad_weight_box,
            grad_bias_box,
            class_part,
            box_part,
        ),
        "roi",
    )
    decoded = lax.dynamic_slice_in_dim(decoded, start_row, share_rows, 1)
    grad_blocks = grad_pooled.reshape(blocks, BLOCK, -1)
    initial_maps = tuple(
        (
            jnp.zeros(
                (channels_here * (SIDE // 2**level_num), images_here * (SIDE // 2**level_num)),
                jnp.float32,
            )
            for level_num in range(4)
        )
    )

    def backward_step(running, pieces):
        return (pool_backward(running, pieces, channels_here, images_here), None)

    maps_grad = lax.scan(
        backward_step, initial_maps, (corner_blocks, image_blocks, level_blocks, grad_blocks)
    )[0]
    pyramid_grads = []
    for level_num in range(4):
        extent = SIDE // 2**level_num
        shaped = (
            maps_grad[level_num]
            .reshape(channels_here, extent, images_here, extent)
            .transpose(2, 0, 1, 3)
        )
        pyramid_grads.append(
            shaped.reshape(images_here, channels_here, extent * extent) * (1.0 / 3.0)
        )
    return (
        class_loss,
        box_loss,
        decoded,
        grad_weight_one,
        grad_bias_one,
        grad_weight_two,
        grad_bias_two,
        grad_weight_class,
        grad_bias_class,
        grad_weight_box,
        grad_bias_box,
        pyramid_grads[0],
        pyramid_grads[1],
        pyramid_grads[2],
        pyramid_grads[3],
    )


def solution(mesh):
    return jax.shard_map(
        on_device,
        mesh=mesh,
        in_specs=(
            P("roi", "ch", None),
            P("roi", "ch", None),
            P("roi", "ch", None),
            P("roi", "ch", None),
            P(None, "roi"),
            P("roi"),
            P("roi"),
            P("roi"),
            P(None, "roi"),
            P("ch", None),
            P(),
            P(),
            P(),
            P(),
            P(),
            P(),
            P(),
        ),
        out_specs=(
            P(),
            P(),
            P(None, ("roi", "ch")),
            P("ch", None),
            P(),
            P(),
            P(),
            P(),
            P(),
            P(),
            P(),
            P("roi", "ch", None),
            P("roi", "ch", None),
            P("roi", "ch", None),
            P("roi", "ch", None),
        ),
        check_vma=False,
    )
```

profile of v0, /device:TPU:4, one launch (start us, length us, event | category | flops | bytes accessed | tf_op | source)
XLA Modules:
  0.0 3560.8 jit_solution(10811847060851008652)
XLA Ops:
  41.6 1792.6 %while.33 = (s32[]{:T(128)}, bf16[4,128,6272]{2,1,0:T(8,128)(2,1)}, s32[4,128]{1,0:T(4,128)S(1)}, s32[4,128]{1,0:T(4,128)S(1)}, f32[4,4,128]{2,1,0:T(4,128)}, /*...) while((s32[]{:T(128)}, bf16[4,128,6272]{2,1,0:T(8,128)(2,1)}, ...), condition=%wide.region_1.2_spmd, body=%wide.region_0.1_spmd.sunk | while | flops 3657506816 | bytes 260893712 | solution.py:228
  58.4 46.4 %reshape.2926 = f32[128,64,128,7]{1,0,3,2:T(8,128)} reshape(f32[8192,896]{0,1:T(8,128)} %convolution_bitcast_fusion.9) | data formatting | bytes 58720256 | tf_op jit(solution)/shard_map/while/body/eval_jaxpr/reshape | solution.py:57
  104.9 61.0 %fusion.209 = f32[128,128,7,7]{1,3,2,0:T(8,128)} fusion(f32[128,64,128,7]{1,0,3,2:T(8,128)} %reshape.2926, f32[128,7]{1,0:T(8,128)S(1)} %copy.252, f32[128,7]{1,0:T(8,128)S(1)} %copy.253), kind=kOutput, calls=%fused_computation.10.clone.2 | convolution fusion | flops 617136128 | bytes 32578560 | tf_op jit(solution)/shard_map/while/body/eval_jaxpr/rih,chrj->rcij/dot_general | solution.py:58
  175.8 34.2 reshape.2927
  210.3 60.9 %fusion.210 = f32[128,128,7,7]{1,3,2,0:T(8,128)} fusion(f32[128,32,128,7]{1,0,3,2:T(8,128)} %reshape.2927, f32[128,7,32,1]{2,1,3,0:T(8,128)S(1)} %copy.256), kind=kOutput, calls=%fused_computation.268.clone.1 | convolution fusion | flops 308281344 | bytes 18006016 | tf_op jit(solution)/shard_map/while/body/eval_jaxpr/rih,chrj->rcij/dot_general | solution.py:58
  277.4 31.9 reshape.2925
  309.7 61.3 %fusion.208 = f32[128,128,7,7]{1,3,2,0:T(8,128)} fusion(f32[128,16,128,7]{1,0,3,2:T(8,128)} %reshape.2925, f32[128,7,16,1]{2,1,3,0:T(8,128)S(1)} %copy.248), kind=kOutput, calls=%fused_computation.269.clone.1 | convolution fusion | flops 154140672 | bytes 10608640 | tf_op jit(solution)/shard_map/while/body/eval_jaxpr/rih,chrj->rcij/dot_general | solution.py:58
  374.5 37.2 %reshape.2928 = f32[128,8,128,7]{1,0,3,2:T(8,128)} reshape(f32[1024,896]{0,1:T(8,128)} %convolution_bitcast_fusion.11) | data formatting | bytes 7340032 | tf_op jit(solution)/shard_map/while/body/eval_jaxpr/reshape | solution.py:57
  411.9 61.3 %fusion.211 = bf16[128,128,7,7]{1,2,3,0:T(8,128)(2,1)} fusion(f32[128,128,7,7]{1,3,2,0:T(8,128)} %fusion.208, f32[128,128,7,7]{1,3,2,0:T(8,128)} %fusion.209, f32[128,128,7,7]{1,3,2,0:T(8,128)} %fusion.210, f32[128,8,128,7]{1,0,3,2:T(8,128)} %reshape.2928, f32[128,7,8,1]{2,1,3,0:T(8,128)S(1)} %copy.258), kind=kOutput, calls=%fused_computation.5.clone.1 | convolution fusion | flops 80281600 | bytes 14938112 | tf_op jit(solution)/shard_map/while/body/eval_jaxpr/rih,chrj->rcij/dot_general | solution.py:58
  504.3 46.4 %reshape.2926 = f32[128,64,128,7]{1,0,3,2:T(8,128)} reshape(f32[8192,896]{0,1:T(8,128)} %convolution_bitcast_fusion.9) | data formatting | bytes 58720256 | tf_op jit(solution)/shard_map/while/body/eval_jaxpr/reshape | solution.py:57
  550.8 61.0 %fusion.209 = f32[128,128,7,7]{1,3,2,0:T(8,128)} fusion(f32[128,64,128,7]{1,0,3,2:T(8,128)} %reshape.2926, f32[128,7]{1,0:T(8,128)S(1)} %copy.252, f32[128,7]{1,0:T(8,128)S(1)} %copy.253), kind=kOutput, calls=%fused_computation.10.clone.2 | convolution fusion | flops 617136128 | bytes 32578560 | tf_op jit(solution)/shard_map/while/body/eval_jaxpr/rih,chrj->rcij/dot_general | solution.py:58
  621.7 34.4 reshape.2927
  656.4 60.9 %fusion.210 = f32[128,128,7,7]{1,3,2,0:T(8,128)} fusion(f32[128,32,128,7]{1,0,3,2:T(8,128)} %reshape.2927, f32[128,7,32,1]{2,1,3,0:T(8,128)S(1)} %copy.256), kind=kOutput, calls=%fused_computation.268.clone.1 | convolution fusion | flops 308281344 | bytes 18006016 | tf_op jit(solution)/shard_map/while/body/eval_jaxpr/rih,chrj->rcij/dot_general | solution.py:58
  723.5 31.9 reshape.2925
  755.7 61.1 %fusion.208 = f32[128,128,7,7]{1,3,2,0:T(8,128)} fusion(f32[128,16,128,7]{1,0,3,2:T(8,128)} %reshape.2925, f32[128,7,16,1]{2,1,3,0:T(8,128)S(1)} %copy.248), kind=kOutput, calls=%fused_computation.269.clone.1 | convolution fusion | flops 154140672 | bytes 10608640 | tf_op jit(solution)/shard_map/while/body/eval_jaxpr/rih,chrj->rcij/dot_general | solution.py:58
  820.4 37.2 %reshape.2928 = f32[128,8,128,7]{1,0,3,2:T(8,128)} reshape(f32[1024,896]{0,1:T(8,128)} %convolution_bitcast_fusion.11) | data formatting | bytes 7340032 | tf_op jit(solution)/shard_map/while/body/eval_jaxpr/reshape | solution.py:57
  857.8 61.4 %fusion.211 = bf16[128,128,7,7]{1,2,3,0:T(8,128)(2,1)} fusion(f32[128,128,7,7]{1,3,2,0:T(8,128)} %fusion.208, f32[128,128,7,7]{1,3,2,0:T(8,128)} %fusion.209, f32[128,128,7,7]{1,3,2,0:T(8,128)} %fusion.210, f32[128,8,128,7]{1,0,3,2:T(8,128)} %reshape.2928, f32[128,7,8,1]{2,1,3,0:T(8,128)S(1)} %copy.258), kind=kOutput, calls=%fused_computation.5.clone.1 | convolution fusion | flops 80281600 | bytes 14938112 | tf_op jit(solution)/shard_map/while/body/eval_jaxpr/rih,chrj->rcij/dot_general | solution.py:58
  950.3 46.4 %reshape.2926 = f32[128,64,128,7]{1,0,3,2:T(8,128)} reshape(f32[8192,896]{0,1:T(8,128)} %convolution_bitcast_fusion.9) | data formatting | bytes 58720256 | tf_op jit(solution)/shard_map/while/body/eval_jaxpr/reshape | solution.py:57
  996.9 61.0 %fusion.209 = f32[128,128,7,7]{1,3,2,0:T(8,128)} fusion(f32[128,64,128,7]{1,0,3,2:T(8,128)} %reshape.2926, f32[128,7]{1,0:T(8,128)S(1)} %copy.252, f32[128,7]{1,0:T(8,128)S(1)} %copy.253), kind=kOutput, calls=%fused_computation.10.clone.2 | convolution fusion | flops 617136128 | bytes 32578560 | tf_op jit(solution)/shard_map/while/body/eval_jaxpr/rih,chrj->rcij/dot_general | solution.py:58
  1067.8 34.2 reshape.2927
  1102.2 60.9 %fusion.210 = f32[128,128,7,7]{1,3,2,0:T(8,128)} fusion(f32[128,32,128,7]{1,0,3,2:T(8,128)} %reshape.2927, f32[128,7,32,1]{2,1,3,0:T(8,128)S(1)} %copy.256), kind=kOutput, calls=%fused_computation.268.clone.1 | convolution fusion | flops 308281344 | bytes 18006016 | tf_op jit(solution)/shard_map/while/body/eval_jaxpr/rih,chrj->rcij/dot_general | solution.py:58
  1169.4 31.9 reshape.2925
  1201.6 61.1 %fusion.208 = f32[128,128,7,7]{1,3,2,0:T(8,128)} fusion(f32[128,16,128,7]{1,0,3,2:T(8,128)} %reshape.2925, f32[128,7,16,1]{2,1,3,0:T(8,128)S(1)} %copy.248), kind=kOutput, calls=%fused_computation.269.clone.1 | convolution fusion | flops 154140672 | bytes 10608640 | tf_op jit(solution)/shard_map/while/body/eval_jaxpr/rih,chrj->rcij/dot_general | solution.py:58
  1266.3 37.2 %reshape.2928 = f32[128,8,128,7]{1,0,3,2:T(8,128)} reshape(f32[1024,896]{0,1:T(8,128)} %convolution_bitcast_fusion.11) | data formatting | bytes 7340032 | tf_op jit(solution)/shard_map/while/body/eval_jaxpr/reshape | solution.py:57
  1303.7 61.6 %fusion.211 = bf16[128,128,7,7]{1,2,3,0:T(8,128)(2,1)} fusion(f32[128,128,7,7]{1,3,2,0:T(8,128)} %fusion.208, f32[128,128,7,7]{1,3,2,0:T(8,128)} %fusion.209, f32[128,128,7,7]{1,3,2,0:T(8,128)} %fusion.210, f32[128,8,128,7]{1,0,3,2:T(8,128)} %reshape.2928, f32[128,7,8,1]{2,1,3,0:T(8,128)S(1)} %copy.258), kind=kOutput, calls=%fused_computation.5.clone.1 | convolution fusion | flops 80281600 | bytes 14938112 | tf_op jit(solution)/shard_map/while/body/eval_jaxpr/rih,chrj->rcij/dot_general | solution.py:58
  1396.2 46.4 %reshape.2926 = f32[128,64,128,7]{1,0,3,2:T(8,128)} reshape(f32[8192,896]{0,1:T(8,128)} %convolution_bitcast_fusion.9) | data formatting | bytes 58720256 | tf_op jit(solution)/shard_map/while/body/eval_jaxpr/reshape | solution.py:57
  1442.8 61.0 %fusion.209 = f32[128,128,7,7]{1,3,2,0:T(8,128)} fusion(f32[128,64,128,7]{1,0,3,2:T(8,128)} %reshape.2926, f32[128,7]{1,0:T(8,128)S(1)} %copy.252, f32[128,7]{1,0:T(8,128)S(1)} %copy.253), kind=kOutput, calls=%fused_computation.10.clone.2 | convolution fusion | flops 617136128 | bytes 32578560 | tf_op jit(solution)/shard_map/while/body/eval_jaxpr/rih,chrj->rcij/dot_general | solution.py:58
  1513.7 34.2 reshape.2927
  1548.2 60.9 %fusion.210 = f32[128,128,7,7]{1,3,2,0:T(8,128)} fusion(f32[128,32,128,7]{1,0,3,2:T(8,128)} %reshape.2927, f32[128,7,32,1]{2,1,3,0:T(8,128)S(1)} %copy.256), kind=kOutput, calls=%fused_computation.268.clone.1 | convolution fusion | flops 308281344 | bytes 18006016 | tf_op jit(solution)/shard_map/while/body/eval_jaxpr/rih,chrj->rcij/dot_general | solution.py:58
  1615.3 31.9 reshape.2925
  1647.5 61.3 %fusion.208 = f32[128,128,7,7]{1,3,2,0:T(8,128)} fusion(f32[128,16,128,7]{1,0,3,2:T(8,128)} %reshape.2925, f32[128,7,16,1]{2,1,3,0:T(8,128)S(1)} %copy.248), kind=kOutput, calls=%fused_computation.269.clone.1 | convolution fusion | flops 154140672 | bytes 10608640 | tf_op jit(solution)/shard_map/while/body/eval_jaxpr/rih,chrj->rcij/dot_general | solution.py:58
  1712.4 37.2 %reshape.2928 = f32[128,8,128,7]{1,0,3,2:T(8,128)} reshape(f32[1024,896]{0,1:T(8,128)} %convolution_bitcast_fusion.11) | data formatting | bytes 7340032 | tf_op jit(solution)/shard_map/while/body/eval_jaxpr/reshape | solution.py:57
  1749.8 61.3 %fusion.211 = bf16[128,128,7,7]{1,2,3,0:T(8,128)(2,1)} fusion(f32[128,128,7,7]{1,3,2,0:T(8,128)} %fusion.208, f32[128,128,7,7]{1,3,2,0:T(8,128)} %fusion.209, f32[128,128,7,7]{1,3,2,0:T(8,128)} %fusion.210, f32[128,8,128,7]{1,0,3,2:T(8,128)} %reshape.2928, f32[128,7,8,1]{2,1,3,0:T(8,128)S(1)} %copy.258), kind=kOutput, calls=%fused_computation.5.clone.1 | convolution fusion | flops 80281600 | bytes 14938112 | tf_op jit(solution)/shard_map/while/body/eval_jaxpr/rih,chrj->rcij/dot_general | solution.py:58
  1847.8 63.6 %all-reduce.5.cloned.1.call-done = f32[512,1024]{1,0:T(8,128)} async-done(((f32[512,1024]{1,0:T(8,128)}), f32[512,1024]{1,0:T(8,128)}) %all-reduce.5.cloned.1.call-update) | async-done | bytes 2097168 | tf_op jit(solution)/shard_map/psum | solution.py:234
  1970.4 1454.2 %while.34 = (s32[]{:T(128)}, f32[8192,128]{1,0:T(8,128)}, f32[4096,64]{0,1:T(8,128)S(1)}, f32[2048,32]{0,1:T(8,128)}, f32[1024,16]{0,1:T(8,128)S(1)}, /*index=5*...) while((s32[]{:T(128)}, f32[8192,128]{1,0:T(8,128)}, ...), condition=%wide.region_23.24_spmd.clone, body=%wide.region_22.23_spmd.clone.sunk | while | flops 3670843392 | bytes 199530736 | solution.py:303
  1985.3 20.5 convert_bitcast_fusion.8
  2005.8 26.8 copy.265
  2032.7 39.6 %reshape.2930 = bf16[8192,896]{0,1:T(8,128)(2,1)} reshape(bf16[128,64,128,7]{1,0,3,2:T(8,128)(2,1)} %copy.265) | data formatting | bytes 29360128 | tf_op jit(solution)/shard_map/while/body/eval_jaxpr/reshape | solution.py:75
  2101.7 23.6 copy.270
  2125.3 36.9 %reshape.2931 = bf16[4096,896]{0,1:T(8,128)(2,1)} reshape(bf16[128,32,128,7]{1,0,3,2:T(8,128)(2,1)} %copy.270) | data formatting | bytes 14680064 | tf_op jit(solution)/shard_map/while/body/eval_jaxpr/reshape | solution.py:75
  2199.5 50.8 %reshape.2932 = bf16[2048,896]{0,1:T(8,128)(2,1)} reshape(bf16[128,16,128,7]{1,0,3,2:T(8,128)(2,1)} %copy.274) | data formatting | bytes 7340032 | tf_op jit(solution)/shard_map/while/body/eval_jaxpr/reshape | solution.py:75
  2283.5 42.6 %reshape.2933 = bf16[1024,896]{0,1:T(8,128)(2,1)} reshape(bf16[128,8,128,7]{1,0,3,2:T(8,128)(2,1)} %copy.279) | data formatting | bytes 3670016 | tf_op jit(solution)/shard_map/while/body/eval_jaxpr/reshape | solution.py:75
  2347.7 20.5 convert_bitcast_fusion.8
  2368.2 26.8 copy.265
  2394.9 39.2 %reshape.2930 = bf16[8192,896]{0,1:T(8,128)(2,1)} reshape(bf16[128,64,128,7]{1,0,3,2:T(8,128)(2,1)} %copy.265) | data formatting | bytes 29360128 | tf_op jit(solution)/shard_map/while/body/eval_jaxpr/reshape | solution.py:75
  2464.8 23.6 copy.270
  2488.4 36.6 %reshape.2931 = bf16[4096,896]{0,1:T(8,128)(2,1)} reshape(bf16[128,32,128,7]{1,0,3,2:T(8,128)(2,1)} %copy.270) | data formatting | bytes 14680064 | tf_op jit(solution)/shard_map/while/body/eval_jaxpr/reshape | solution.py:75
  2562.3 51.0 %reshape.2932 = bf16[2048,896]{0,1:T(8,128)(2,1)} reshape(bf16[128,16,128,7]{1,0,3,2:T(8,128)(2,1)} %copy.274) | data formatting | bytes 7340032 | tf_op jit(solution)/shard_map/while/body/eval_jaxpr/reshape | solution.py:75
  2646.5 42.6 %reshape.2933 = bf16[1024,896]{0,1:T(8,128)(2,1)} reshape(bf16[128,8,128,7]{1,0,3,2:T(8,128)(2,1)} %copy.279) | data formatting | bytes 3670016 | tf_op jit(solution)/shard_map/while/body/eval_jaxpr/reshape | solution.py:75
  2710.3 20.5 convert_bitcast_fusion.8
  2730.8 26.6 copy.265
  2757.5 38.7 %reshape.2930 = bf16[8192,896]{0,1:T(8,128)(2,1)} reshape(bf16[128,64,128,7]{1,0,3,2:T(8,128)(2,1)} %copy.265) | data formatting | bytes 29360128 | tf_op jit(solution)/shard_map/while/body/eval_jaxpr/reshape | solution.py:75
  2826.6 23.7 copy.270
  2850.3 36.6 %reshape.2931 = bf16[4096,896]{0,1:T(8,128)(2,1)} reshape(bf16[128,32,128,7]{1,0,3,2:T(8,128)(2,1)} %copy.270) | data formatting | bytes 14680064 | tf_op jit(solution)/shard_map/while/body/eval_jaxpr/reshape | solution.py:75
  2924.2 50.8 %reshape.2932 = bf16[2048,896]{0,1:T(8,128)(2,1)} reshape(bf16[128,16,128,7]{1,0,3,2:T(8,128)(2,1)} %copy.274) | data formatting | bytes 7340032 | tf_op jit(solution)/shard_map/while/body/eval_jaxpr/reshape | solution.py:75
  3008.2 42.6 %reshape.2933 = bf16[1024,896]{0,1:T(8,128)(2,1)} reshape(bf16[128,8,128,7]{1,0,3,2:T(8,128)(2,1)} %copy.279) | data formatting | bytes 3670016 | tf_op jit(solution)/shard_map/while/body/eval_jaxpr/reshape | solution.py:75
  3072.1 20.5 convert_bitcast_fusion.8
  3092.6 26.6 copy.265
  3119.2 38.9 %reshape.2930 = bf16[8192,896]{0,1:T(8,128)(2,1)} reshape(bf16[128,64,128,7]{1,0,3,2:T(8,128)(2,1)} %copy.265) | data formatting | bytes 29360128 | tf_op jit(solution)/shard_map/while/body/eval_jaxpr/reshape | solution.py:75
  3188.5 23.5 copy.270
  3212.0 36.6 %reshape.2931 = bf16[4096,896]{0,1:T(8,128)(2,1)} reshape(bf16[128,32,128,7]{1,0,3,2:T(8,128)(2,1)} %copy.270) | data formatting | bytes 14680064 | tf_op jit(solution)/shard_map/while/body/eval_jaxpr/reshape | solution.py:75
  3285.9 50.8 %reshape.2932 = bf16[2048,896]{0,1:T(8,128)(2,1)} reshape(bf16[128,16,128,7]{1,0,3,2:T(8,128)(2,1)} %copy.274) | data formatting | bytes 7340032 | tf_op jit(solution)/shard_map/while/body/eval_jaxpr/reshape | solution.py:75
  3369.9 42.6 %reshape.2933 = bf16[1024,896]{0,1:T(8,128)(2,1)} reshape(bf16[128,8,128,7]{1,0,3,2:T(8,128)(2,1)} %copy.279) | data formatting | bytes 3670016 | tf_op jit(solution)/shard_map/while/body/eval_jaxpr/reshape | solution.py:75
  3428.1 56.4 %all-reduce = (f32[]{:T(128)}, f32[]{:T(128)}, f32[1024]{0:T(1024)}, f32[1024]{0:T(1024)}, f32[81]{0:T(128)}, /*index=5*/f32[1024,4]{0,1:T(4,128)}, f32[4]{0:T(128)}) all-reduce(f32[]{:T(128)S(6)} %div.186, f32[]{:T(128)S(6)} %div.187, f32[1024]{0:T(1024)S(1)} %copy-done.31, ...), channel_id=1, replica_groups=mesh['roi'=16,'ch'=2] {'roi'}, use_global_device_ids=true, to_apply=%region_7.8 | all-reduce | flops 6231 | bytes 49848 | tf_op jit(solution)/shard_map/psum | solution.py:273
  (591 shorter events, 869.6 us)
Async XLA Ops:
  7.2 1910.1 %copy-start = (bf16[1024,1024]{1,0:T(8,128)(2,1)S(1)}, bf16[1024,1024]{1,0:T(8,128)(2,1)}, u32[]{:S(2)}) copy-start(bf16[1024,1024]{1,0:T(8,128)(2,1)} %param.32) | copy-start | bytes 6291460
  7.2 1904.2 %all-reduce.5.cloned.1.call-start = ((), (), s32[]{:S(2)}) async-start(), calls=%async_computation | async-start | bytes 4194304 | tf_op jit(solution)/shard_map/psum | solution.py:234
  20.9 7.9 copy-start.7
  32.8 4.8 copy-start.13
  37.6 2.4 copy-start.19
  37.6 4.0 copy-start.36
  37.6 4.0 copy-start.25
  41.8 2.1 copy-start.37
  309.6 61.3 %copy-start.10 = (f32[128,7]{0,1:T(8,128)S(1)}, f32[128,7]{0,1:T(8,128)}, u32[]{:S(2)}) copy-start(f32[128,7]{0,1:T(8,128)} %get-tuple-element.1008) | copy-start | bytes 10756 | tf_op jit(solution)/shard_map/while
  309.6 61.3 %copy-start.11 = (f32[128,7]{0,1:T(8,128)S(1)}, f32[128,7]{0,1:T(8,128)}, u32[]{:S(2)}) copy-start(f32[128,7]{0,1:T(8,128)} %get-tuple-element.1007) | copy-start | bytes 10756 | tf_op jit(solution)/shard_map/while
  309.6 61.6 %copy-start.14 = (f32[2,128]{1,0:T(2,128)S(1)}, f32[2,128]{1,0:T(2,128)}, u32[]{:S(2)}) copy-start(f32[2,128]{1,0:T(2,128)} %get-tuple-element.1009) | copy-start | bytes 3076 | tf_op jit(solution)/shard_map/while
  374.5 37.2 %copy-start.8 = (f32[128,7]{0,1:T(8,128)S(1)}, f32[128,7]{0,1:T(8,128)}, u32[]{:S(2)}) copy-start(f32[128,7]{0,1:T(8,128)} %get-tuple-element.1010) | copy-start | bytes 10756 | tf_op jit(solution)/shard_map/while
  374.5 37.2 %copy-start.9 = (f32[128,7]{0,1:T(8,128)S(1)}, f32[128,7]{0,1:T(8,128)}, u32[]{:S(2)}) copy-start(f32[128,7]{0,1:T(8,128)} %get-tuple-element.1011) | copy-start | bytes 10756 | tf_op jit(solution)/shard_map/while
  484.7 2.7 copy-start.26
  484.7 2.7 copy-start.38
  487.7 2.1 copy-start.37
  755.7 61.1 %copy-start.10 = (f32[128,7]{0,1:T(8,128)S(1)}, f32[128,7]{0,1:T(8,128)}, u32[]{:S(2)}) copy-start(f32[128,7]{0,1:T(8,128)} %get-tuple-element.1008) | copy-start | bytes 10756 | tf_op jit(solution)/shard_map/while
  755.7 61.1 %copy-start.11 = (f32[128,7]{0,1:T(8,128)S(1)}, f32[128,7]{0,1:T(8,128)}, u32[]{:S(2)}) copy-start(f32[128,7]{0,1:T(8,128)} %get-tuple-element.1007) | copy-start | bytes 10756 | tf_op jit(solution)/shard_map/while
  755.7 61.4 %copy-start.14 = (f32[2,128]{1,0:T(2,128)S(1)}, f32[2,128]{1,0:T(2,128)}, u32[]{:S(2)}) copy-start(f32[2,128]{1,0:T(2,128)} %get-tuple-element.1009) | copy-start | bytes 3076 | tf_op jit(solution)/shard_map/while
  816.8 1.1 copy-start.5
  820.4 37.2 %copy-start.8 = (f32[128,7]{0,1:T(8,128)S(1)}, f32[128,7]{0,1:T(8,128)}, u32[]{:S(2)}) copy-start(f32[128,7]{0,1:T(8,128)} %get-tuple-element.1010) | copy-start | bytes 10756 | tf_op jit(solution)/shard_map/while
  820.4 37.2 %copy-start.9 = (f32[128,7]{0,1:T(8,128)S(1)}, f32[128,7]{0,1:T(8,128)}, u32[]{:S(2)}) copy-start(f32[128,7]{0,1:T(8,128)} %get-tuple-element.1011) | copy-start | bytes 10756 | tf_op jit(solution)/shard_map/while
  930.6 2.7 copy-start.26
  930.6 2.7 copy-start.38
  933.7 2.1 copy-start.37
  1201.6 61.2 %copy-start.10 = (f32[128,7]{0,1:T(8,128)S(1)}, f32[128,7]{0,1:T(8,128)}, u32[]{:S(2)}) copy-start(f32[128,7]{0,1:T(8,128)} %get-tuple-element.1008) | copy-start | bytes 10756 | tf_op jit(solution)/shard_map/while
  1201.6 61.1 %copy-start.11 = (f32[128,7]{0,1:T(8,128)S(1)}, f32[128,7]{0,1:T(8,128)}, u32[]{:S(2)}) copy-start(f32[128,7]{0,1:T(8,128)} %get-tuple-element.1007) | copy-start | bytes 10756 | tf_op jit(solution)/shard_map/while
  1201.6 61.4 %copy-start.14 = (f32[2,128]{1,0:T(2,128)S(1)}, f32[2,128]{1,0:T(2,128)}, u32[]{:S(2)}) copy-start(f32[2,128]{1,0:T(2,128)} %get-tuple-element.1009) | copy-start | bytes 3076 | tf_op jit(solution)/shard_map/while
  1266.3 37.2 %copy-start.8 = (f32[128,7]{0,1:T(8,128)S(1)}, f32[128,7]{0,1:T(8,128)}, u32[]{:S(2)}) copy-start(f32[128,7]{0,1:T(8,128)} %get-tuple-element.1010) | copy-start | bytes 10756 | tf_op jit(solution)/shard_map/while
  1266.3 37.2 %copy-start.9 = (f32[128,7]{0,1:T(8,128)S(1)}, f32[128,7]{0,1:T(8,128)}, u32[]{:S(2)}) copy-start(f32[128,7]{0,1:T(8,128)} %get-tuple-element.1011) | copy-start | bytes 10756 | tf_op jit(solution)/shard_map/while
  1376.7 2.8 copy-start.26
  1376.7 2.8 copy-start.38
  1379.6 2.1 copy-start.37
  1647.5 61.3 %copy-start.10 = (f32[128,7]{0,1:T(8,128)S(1)}, f32[128,7]{0,1:T(8,128)}, u32[]{:S(2)}) copy-start(f32[128,7]{0,1:T(8,128)} %get-tuple-element.1008) | copy-start | bytes 10756 | tf_op jit(solution)/shard_map/while
  1647.5 61.3 %copy-start.11 = (f32[128,7]{0,1:T(8,128)S(1)}, f32[128,7]{0,1:T(8,128)}, u32[]{:S(2)}) copy-start(f32[128,7]{0,1:T(8,128)} %get-tuple-element.1007) | copy-start | bytes 10756 | tf_op jit(solution)/shard_map/while
  1647.5 61.6 %copy-start.14 = (f32[2,128]{1,0:T(2,128)S(1)}, f32[2,128]{1,0:T(2,128)}, u32[]{:S(2)}) copy-start(f32[2,128]{1,0:T(2,128)} %get-tuple-element.1009) | copy-start | bytes 3076 | tf_op jit(solution)/shard_map/while
  1712.4 37.2 %copy-start.8 = (f32[128,7]{0,1:T(8,128)S(1)}, f32[128,7]{0,1:T(8,128)}, u32[]{:S(2)}) copy-start(f32[128,7]{0,1:T(8,128)} %get-tuple-element.1010) | copy-start | bytes 10756 | tf_op jit(solution)/shard_map/while
  1712.4 37.2 %copy-start.9 = (f32[128,7]{0,1:T(8,128)S(1)}, f32[128,7]{0,1:T(8,128)}, u32[]{:S(2)}) copy-start(f32[128,7]{0,1:T(8,128)} %get-tuple-element.1011) | copy-start | bytes 10756 | tf_op jit(solution)/shard_map/while
  1822.6 2.7 copy-start.26
  1822.6 2.7 copy-start.38
  1834.2 12.9 copy-start.39
  1847.1 1685.0 %all-reduce.7.cloned.1.call-start = ((), (), s32[]{:S(2)}) async-start(), calls=%async_computation.1 | async-start | bytes 60489728 | tf_op jit(solution)/shard_map/psum | solution.py:273
  1917.3 12.0 copy-start.6
  1929.2 3.3 copy-start.1
  1929.7 2.8 copy-start.16
  1930.4 3.8 copy-start.21
  1930.4 2.2 copy-start.27
  1930.4 2.2 copy-start.28
  1934.2 1.9 copy-start.23
  1936.1 3.3 copy-start.4
  1936.1 6.9 slice-start
  1939.5 3.6 slice-start.1
  1970.3 1454.3 %copy-start.17 = (f32[512]{0:T(512)S(1)}, f32[512]{0:T(512)}, u32[]{:S(2)}) copy-start(f32[512]{0:T(512)} %copy-done.16) | copy-start | bytes 6148
  1970.4 1454.3 %copy-start.22 = (f32[512]{0:T(512)S(1)}, f32[512]{0:T(512)}, u32[]{:S(2)}) copy-start(f32[512]{0:T(512)} %copy-done.21) | copy-start | bytes 6148
  1970.4 1454.3 %copy-start.29 = (f32[512]{0:T(512)S(1)}, f32[512]{0:T(512)}, u32[]{:S(2)}) copy-start(f32[512]{0:T(512)} %get-tuple-element.487) | copy-start | bytes 6148
  1970.4 1456.2 %copy-start.24 = (bf16[512,4]{0,1:T(4,128)(2,1)S(1)}, bf16[512,4]{0,1:T(4,128)(2,1)}, u32[]{:S(2)}) copy-start(bf16[512,4]{0,1:T(4,128)(2,1)} %copy-done.23) | copy-start | bytes 12292
  1970.4 1457.7 %copy-start.30 = (f32[1024]{0:T(1024)S(1)}, f32[1024]{0:T(1024)}, u32[]{:S(2)}) copy-start(f32[1024]{0:T(1024)} %get-tuple-element.774) | copy-start | bytes 12292
  1970.4 1457.7 %copy-start.31 = (f32[1024]{0:T(1024)S(1)}, f32[1024]{0:T(1024)}, u32[]{:S(2)}) copy-start(f32[1024]{0:T(1024)} %get-tuple-element.556) | copy-start | bytes 12292
  1970.4 1457.7 %copy-start.34 = (f32[81]{0:T(128)S(1)}, f32[81]{0:T(128)}, u32[]{:S(2)}) copy-start(f32[81]{0:T(128)} %get-tuple-element.554) | copy-start | bytes 976
  1970.4 1457.6 %copy-start.35 = (f32[4]{0:T(128)S(1)}, f32[4]{0:T(128)}, u32[]{:S(2)}) copy-start(f32[4]{0:T(128)} %get-tuple-element.552) | copy-start | bytes 52
  3523.4 1.3 copy-start.2
  3526.8 4.6 copy-start.18
  3532.1 18.5 copy-start.3
  3550.7 2.0 copy-start.12
  (10 other events, 8.3 us)
Sparse Core Ops, SparseCore 0:
  1847.3 64.0 all-reduce.4
  1969.8 517.5 all-reduce.6
where the time goes:
time: 3610 us; the launch traced here: 3560 us
  local copies, waits for them, and re-layouts  1920 us (53%)
  matrix products  1420 us (39%)
  other arithmetic  70.5 us (2%)
  waiting for transfers between devices  63.6 us (2%)
  blocking collectives  56.4 us (2%)
    dot_general x16, matrix products, pool_forward(): jnp.einsum('rih,chrj->rcij', downward, section_one, precision=lax.Precisi...  978 us
    reshape x16, local copies, waits for them, and re-layouts, pool_backward(): grad_section.astype(jnp.bfloat16)  677 us
    reshape x16, local copies, waits for them, and re-layouts, pool_forward(): section_one = section_one.reshape(channels_here, extent, region_count, POOL)  599 us
    convert_element_type x16, local copies, waits for them, and re-layouts, pool_backward(): grad_section.astype(jnp.bfloat16)  360 us
    dot_general x16, matrix products, pool_backward(): jnp.einsum('rih,rcij->chrj', downward, grad_cells, precision=lax.Precisio...  169 us
    dot_general x16, matrix products, pool_forward(): jnp.dot(matrices[level_num], select, preferred_element_type=jnp.float32)  119 us
    dot_general x16, matrix products, pool_backward(): lax.dot_general(grad_section, select, (((1,), (1,)), ((), ())), preferred...  89.2 us
  transfers between devices with their start and end apart: 2, of which 1 were waited for; matrix products, arithmetic and copies ran while one was open for 42% of the time, Pallas kernels for 0%

commit v1 on v0

v1 whole, which is shorter than its diff:
```python
import functools
import jax, jax.numpy as jnp
from jax import lax
from jax.sharding import PartitionSpec as P
from jax.experimental import pallas as pl
from jax.experimental.pallas import tpu as pltpu

POOL = 7
SAMPLES = 2
SIDE = 64
LANES = 128
BF = jnp.bfloat16
F32 = jnp.float32
VM = 60 * 2**20


def spread(low, high, extent):
    anchor = low * extent - 0.5
    stride = (high - low) * extent / POOL
    places = lax.broadcasted_iota(jnp.int32, (extent, LANES), 0).astype(F32)
    out = []
    for col in range(POOL):
        total = None
        for s in range(SAMPLES):
            at = jnp.clip(anchor + (col + (s + 0.5) / SAMPLES) * stride, 0.0, extent - 1.0)
            term = jnp.maximum(0.0, 1.0 - jnp.abs(at - places))
            total = term if total is None else total + term
        out.append(total / SAMPLES)
    return out


def write_tables(across_ref, down_ref, rows, extent, level):
    x1, y1, x2, y2 = (rows[k : k + 1] for k in range(4))
    mask = (rows[9:10] == float(level)).astype(F32)
    across = spread(x1, x2, extent)
    down = spread(y1, y2, extent)
    for j in range(POOL):
        a = (across[j] * mask).astype(BF).astype(F32)
        if extent < 16:
            a = jnp.concatenate([a] * (16 // extent), 0)
        across_ref[j, :, :] = a.astype(BF)
    for i in range(POOL):
        d = down[i]
        if extent < 16:
            half = lax.broadcasted_iota(jnp.int32, (16, LANES), 0) < extent
            for q in range(extent // 2):
                top = jnp.broadcast_to(d[2 * q : 2 * q + 1], (16, LANES))
                low = jnp.broadcast_to(d[2 * q + 1 : 2 * q + 2], (16, LANES))
                down_ref[i, q] = jnp.where(half, top, low).astype(BF)
        else:
            for h in range(extent):
                down_ref[i, h] = jnp.broadcast_to(d[h : h + 1], (16, LANES)).astype(BF)


def kernel_row(k_ref, across_ref, down_ref, i, extent):
    wide = max(extent, 16)
    tiles = extent if extent >= 16 else extent // 2

    def body(q, c):
        d = down_ref[i, q]
        for j in range(POOL):
            for v in range(wide // 16):
                k_ref[pl.ds(pl.multiple_of(q * wide + v * 16, 16), 16), j * LANES : (j + 1) * LANES] = (
                    across_ref[j, v * 16 : (v + 1) * 16, :] * d
                )
        return c

    lax.fori_loop(0, tiles, body, 0, unroll=min(tiles, 8))


def sort_tables(table):
    n = table.shape[1]
    level = table[9:10]
    which = lax.broadcasted_iota(jnp.int32, (8, n), 0).astype(F32)
    onehot = (level == which).astype(F32)
    before = (
        lax.broadcasted_iota(jnp.int32, (n, n), 0) < lax.broadcasted_iota(jnp.int32, (n, n), 1)
    ).astype(BF)
    earlier = jnp.dot(onehot.astype(BF), before, preferred_element_type=F32)
    lower = (which < level).astype(F32) * 1.0
    counts = jnp.sum(onehot, axis=1, keepdims=True)
    rank = jnp.sum(onehot * earlier + lower * counts, axis=0, keepdims=True)
    return rank


def permute(table, rank):
    n = table.shape[1]
    place = lax.broadcasted_iota(jnp.int32, (n, n), 0).astype(F32)
    q = (rank == place).astype(F32)
    return lax.dot_general(
        table, q, (((1,), (1,)), ((), ())), precision=lax.Precision.HIGHEST, preferred_element_type=F32
    )


def forward_kernel(table_ref, p2, p3, p4, p5, out_ref, sorted_ref, acc, acr, dwn, kbuf, *, channels):
    pyr = (p2, p3, p4, p5)
    tile = pl.program_id(0)

    @pl.when(tile == 0)
    def _():
        table = table_ref[...]
        rank = sort_tables(table)
        full = permute(table, rank)
        sorted_ref[0:16, :] = full
        sorted_ref[16:24, :] = jnp.broadcast_to(rank, (8, table.shape[1]))

    rows = sorted_ref[0:16, pl.ds(pl.multiple_of(tile * LANES, LANES), LANES)]
    acc[...] = jnp.zeros_like(acc)
    first = rows[8:9] == 0.0
    cells = POOL * POOL
    for level in range(4):
        extent = SIDE // 2**level
        size = extent * extent
        here = jnp.sum((rows[9:10] == float(level)).astype(F32)) > 0.0

        @pl.when(here)
        def _():
            wide = max(extent, 16)
            a_ref = acr.at[:, 0:wide, :]
            write_tables(a_ref, dwn, rows, extent, level)
            k_ref = kbuf.at[0:size, :]

            def row(i, c):
                kernel_row(k_ref, a_ref, dwn, i, extent)
                got = jnp.dot(pyr[level][...], k_ref[...], preferred_element_type=F32)
                sel = jnp.where(
                    jnp.concatenate([first] * POOL, 1), got[:channels], got[channels:]
                )
                for j in range(POOL):
                    at = pl.ds(i * POOL + j, channels, stride=cells)
                    acc[at, :] = acc[at, :] + sel[:, j * LANES : (j + 1) * LANES]
                return c

            lax.fori_loop(0, POOL, row, 0)

    out_ref[...] = acc[...].astype(BF)


def pool_forward(table, maps, channels):
    n = table.shape[1]
    flat = channels * POOL * POOL
    full = lambda a: pl.BlockSpec(a.shape, lambda t: (0,) * a.ndim)
    return pl.pallas_call(
        functools.partial(forward_kernel, channels=channels),
        grid=(n // LANES,),
        in_specs=[full(table)] + [full(m) for m in maps],
        out_specs=[
            pl.BlockSpec((flat, LANES), lambda t: (0, t)),
            pl.BlockSpec((24, n), lambda t: (0, 0)),
        ],
        out_shape=[
            jax.ShapeDtypeStruct((flat, n), BF),
            jax.ShapeDtypeStruct((24, n), F32),
        ],
        scratch_shapes=[
            pltpu.VMEM((flat, LANES), F32),
            pltpu.VMEM((POOL, SIDE, LANES), BF),
            pltpu.VMEM((POOL, SIDE, 16, LANES), BF),
            pltpu.VMEM((SIDE * SIDE, POOL * LANES), BF),
        ],
        compiler_params=pltpu.CompilerParams(vmem_limit_bytes=VM),
        name="pool_forward",
    )(table, *maps)


def backward_kernel(sorted_ref, gp_ref, o2, o3, o4, o5, g32, acr, dwn, kbuf, gbuf, *, channels):
    outs = (o2, o3, o4, o5)
    tile = pl.program_id(0)

    @pl.when(tile == 0)
    def _():
        for o in outs:
            o[...] = jnp.zeros_like(o)

    rows = sorted_ref[0:16, pl.ds(pl.multiple_of(tile * LANES, LANES), LANES)]
    g32[...] = gp_ref[...].astype(F32) * (1.0 / 3.0)
    first = rows[8:9] == 0.0
    cells = POOL * POOL
    for level in range(4):
        extent = SIDE // 2**level
        size = extent * extent
        here = jnp.sum((rows[9:10] == float(level)).astype(F32)) > 0.0

        @pl.when(here)
        def _():
            wide = max(extent, 16)
            a_ref = acr.at[:, 0:wide, :]
            write_tables(a_ref, dwn, rows, extent, level)
            k_ref = kbuf.at[0:size, :]

            def row(i, c):
                kernel_row(k_ref, a_ref, dwn, i, extent)
                for j in range(POOL):
                    g = g32[pl.ds(i * POOL + j, channels, stride=cells), :]
                    gbuf[0:channels, j * LANES : (j + 1) * LANES] = jnp.where(first, g, 0.0).astype(BF)
                    gbuf[channels:, j * LANES : (j + 1) * LANES] = jnp.where(first, 0.0, g).astype(BF)
                outs[level][...] += lax.dot_general(
                    gbuf[...], k_ref[...], (((1,), (1,)), ((), ())), preferred_element_type=F32
                )
                return c

            lax.fori_loop(0, POOL, row, 0)


def pool_backward(sorted_table, gp, channels):
    n = sorted_table.shape[1]
    flat = channels * POOL * POOL
    sizes = [(SIDE // 2**l) ** 2 for l in range(4)]
    return pl.pallas_call(
        functools.partial(backward_kernel, channels=channels),
        grid=(n // LANES,),
        in_specs=[
            pl.BlockSpec(sorted_table.shape, lambda t: (0, 0)),
            pl.BlockSpec((flat, LANES), lambda t: (0, t)),
        ],
        out_specs=[pl.BlockSpec((2 * channels, s), lambda t: (0, 0)) for s in sizes],
        out_shape=[jax.ShapeDtypeStruct((2 * channels, s), F32) for s in sizes],
        scratch_shapes=[
            pltpu.VMEM((flat, LANES), F32),
            pltpu.VMEM((POOL, SIDE, LANES), BF),
            pltpu.VMEM((POOL, SIDE, 16, LANES), BF),
            pltpu.VMEM((SIDE * SIDE, POOL * LANES), BF),
            pltpu.VMEM((2 * channels, POOL * LANES), BF),
        ],
        compiler_params=pltpu.CompilerParams(vmem_limit_bytes=VM),
        name="pool_backward",
    )(sorted_table, gp)


def decode_boxes(corners, deltas):
    widths = corners[2] - corners[0]
    heights = corners[3] - corners[1]
    centre_x = corners[0] + 0.5 * widths
    centre_y = corners[1] + 0.5 * heights
    moved_x = deltas[:, 0] / 10.0 * widths + centre_x
    moved_y = deltas[:, 1] / 10.0 * heights + centre_y
    new_width = jnp.exp(deltas[:, 2] / 5.0) * widths
    new_height = jnp.exp(deltas[:, 3] / 5.0) * heights
    return jnp.stack(
        [
            moved_x - 0.5 * new_width,
            moved_y - 0.5 * new_height,
            moved_x + 0.5 * new_width,
            moved_y + 0.5 * new_height,
        ]
    )


def column_sums(matrix):
    return jnp.sum(matrix.astype(jnp.float32), axis=0)


def transposed_product(left_rows, right_rows):
    return lax.dot_general(
        left_rows, right_rows, (((0,), (0,)), ((), ())), preferred_element_type=jnp.float32
    )


def product_with_transpose(left_rows, right_rows):
    return lax.dot_general(
        left_rows, right_rows, (((1,), (1,)), ((), ())), preferred_element_type=jnp.float32
    )


def head_pass(
    summed,
    first_bias,
    second_weight,
    second_bias,
    class_weight,
    class_bias,
    box_weight,
    box_bias,
    label_rows,
    target_rows,
    corner_rows,
    norm_count,
):
    pre_one = summed + first_bias.astype(jnp.float32)
    act_one, gelu_one = jax.vjp(smooth_unit, pre_one)
    act_one = act_one.astype(jnp.bfloat16)
    pre_two = jnp.dot(
        act_one, second_weight, preferred_element_type=jnp.float32
    ) + second_bias.astype(jnp.float32)
    act_two, gelu_two = jax.vjp(smooth_unit, pre_two)
    act_two = act_two.astype(jnp.bfloat16)
    logits = jnp.dot(act_two, class_weight, preferred_element_type=jnp.float32) + class_bias.astype(
        jnp.float32
    )
    deltas = jnp.dot(act_two, box_weight, preferred_element_type=jnp.float32) + box_bias.astype(
        jnp.float32
    )
    classes = logits.shape[1]
    row_max = jnp.max(logits, axis=1, keepdims=True)
    exponent = jnp.exp(logits - row_max)
    row_total = jnp.sum(exponent, axis=1, keepdims=True)
    onehot = (label_rows[:, None] == jnp.arange(classes, dtype=jnp.int32)[None, :]).astype(
        jnp.float32
    )
    class_part = (
        jnp.sum(row_max[:, 0] + jnp.log(row_total[:, 0]) - jnp.sum(logits * onehot, axis=1))
        / norm_count
    )
    foreground = (label_rows < classes - 1).astype(jnp.float32)[:, None]
    residue = deltas - target_rows.T
    magnitude = jnp.abs(residue)
    huber = jnp.where(magnitude < 1.0, 0.5 * residue * residue, magnitude - 0.5)
    box_part = jnp.sum(foreground * huber) / norm_count
    grad_logits = ((exponent / row_total - onehot) / norm_count).astype(jnp.bfloat16)
    grad_deltas = (foreground * jnp.clip(residue, -1.0, 1.0) / norm_count).astype(jnp.bfloat16)
    grad_weight_class = transposed_product(act_two, grad_logits)
    grad_bias_class = column_sums(grad_logits)
    grad_weight_box = transposed_product(act_two, grad_deltas)
    grad_bias_box = column_sums(grad_deltas)
    grad_act_two = product_with_transpose(grad_logits, class_weight) + product_with_transpose(
        grad_deltas, box_weight
    )
    grad_pre_two = gelu_two(grad_act_two)[0].astype(jnp.bfloat16)
    grad_weight_two = transposed_product(act_one, grad_pre_two)
    grad_bias_two = column_sums(grad_pre_two)
    grad_act_one = product_with_transpose(grad_pre_two, second_weight)
    grad_pre_one = gelu_one(grad_act_one)[0].astype(jnp.bfloat16)
    grad_bias_one = column_sums(grad_pre_one)
    decoded = decode_boxes(corner_rows, deltas)
    small_grads = (
        grad_bias_one,
        grad_weight_two,
        grad_bias_two,
        grad_weight_class,
        grad_bias_class,
        grad_weight_box,
        grad_bias_box,
        class_part,
        box_part,
    )
    return (grad_pre_one, small_grads, decoded)


def smooth_unit(values):
    return jax.nn.gelu(values, approximate=False)


def on_device(
    pyramid_two,
    pyramid_three,
    pyramid_four,
    pyramid_five,
    proposals,
    image_index,
    levels,
    labels,
    targets,
    first_weight,
    first_bias,
    second_weight,
    second_bias,
    class_weight,
    class_bias,
    box_weight,
    box_bias,
):
    features = (pyramid_two, pyramid_three, pyramid_four, pyramid_five)
    images_here, channels_here = (pyramid_two.shape[0], pyramid_two.shape[1])
    regions_here = proposals.shape[1]
    local_image = image_index - lax.axis_index("roi") * images_here
    maps = [f.reshape(images_here * channels_here, -1) for f in features]
    table = jnp.concatenate(
        [
            proposals,
            targets,
            local_image[None].astype(F32),
            levels[None].astype(F32),
            labels[None].astype(F32),
            jnp.zeros((5, regions_here), F32),
        ]
    )
    pooled, ordered = pool_forward(table, maps, channels_here)
    norm_count = float(regions_here * lax.axis_size("roi"))
    partial = lax.dot_general(
        pooled, first_weight, (((0,), (0,)), ((), ())), preferred_element_type=F32
    )
    if lax.axis_size("ch") == 2:
        partial = partial.astype(BF)
        other = lax.ppermute(partial, "ch", [(0, 1), (1, 0)])
        summed = partial.astype(F32) + other.astype(F32)
    else:
        summed = lax.psum(partial, "ch")
    grad_pre_one, small_grads, decoded = head_pass(
        summed,
        first_bias,
        second_weight,
        second_bias,
        class_weight,
        class_bias,
        box_weight,
        box_bias,
        ordered[10].astype(jnp.int32),
        ordered[4:8],
        ordered[0:4],
        norm_count,
    )
    grad_weight_one = lax.dot_general(
        pooled, grad_pre_one, (((1,), (0,)), ((), ())), preferred_element_type=F32
    ).astype(BF)
    grad_pooled = lax.dot_general(
        first_weight, grad_pre_one, (((1,), (1,)), ((), ())), preferred_element_type=F32
    ).astype(BF)
    grad_weight_one, grad_weight_two = lax.psum((grad_weight_one, small_grads[1].astype(BF)), "roi")
    small = lax.psum(small_grads[0:1] + small_grads[2:], "roi")
    grad_bias_one, grad_bias_two, grad_weight_class, grad_bias_class, grad_weight_box, grad_bias_box, class_loss, box_loss = small
    rank = ordered[16]
    place = jnp.arange(regions_here, dtype=F32)
    back = (place[:, None] == rank[None, :]).astype(F32)
    decoded = jnp.dot(decoded, back, precision=lax.Precision.HIGHEST)
    share_rows = regions_here // lax.axis_size("ch")
    decoded = lax.dynamic_slice_in_dim(decoded, lax.axis_index("ch") * share_rows, share_rows, 1)
    map_grads = pool_backward(ordered, grad_pooled, channels_here)
    pyramid_grads = [g.reshape(f.shape) for g, f in zip(map_grads, features)]
    return (
        class_loss,
        box_loss,
        decoded,
        grad_weight_one.astype(F32),
        grad_bias_one,
        grad_weight_two.astype(F32),
        grad_bias_two,
        grad_weight_class,
        grad_bias_class,
        grad_weight_box,
        grad_bias_box,
        pyramid_grads[0],
        pyramid_grads[1],
        pyramid_grads[2],
        pyramid_grads[3],
    )


def solution(mesh):
    return jax.shard_map(
        on_device,
        mesh=mesh,
        in_specs=(
            P("roi", "ch", None),
            P("roi", "ch", None),
            P("roi", "ch", None),
            P("roi", "ch", None),
            P(None, "roi"),
            P("roi"),
            P("roi"),
            P("roi"),
            P(None, "roi"),
            P("ch", None),
            P(),
            P(),
            P(),
            P(),
            P(),
            P(),
            P(),
        ),
        out_specs=(
            P(),
            P(),
            P(None, ("roi", "ch")),
            P("ch", None),
            P(),
            P(),
            P(),
            P(),
            P(),
            P(),
            P(),
            P("roi", "ch", None),
            P("roi", "ch", None),
            P("roi", "ch", None),
            P("roi", "ch", None),
        ),
        check_vma=False,
    )
```

time: 3610 us -> 543 us (0.15); the launches traced: 3560 us -> 538 us
  local copies, waits for them, and re-layouts: 1920 us -> 7.46 us
  matrix products: 1420 us -> 55.8 us
  Pallas kernels: 0 us -> 163 us
  waiting for transfers between devices: 63.6 us -> 208 us
  other arithmetic: 70.5 us -> 28.6 us
    dot_general x65 -> x4, matrix products: 1370 us -> 35.8 us  [the longest x1 13.5 us: on_device(): lax.dot_general(first_weight, grad_pre_one, (((1,), (1,)), ((), ())), pre...]
    reshape x42 -> x0, local copies, waits for them, and re-layouts: 1310 us -> none  [the longest x16 677 us: pool_backward(): grad_section.astype(jnp.bfloat16)]
    convert_element_type x80 -> x0, local copies, waits for them, and re-layouts: 420 us -> none  [the longest x16 360 us: pool_backward(): grad_section.astype(jnp.bfloat16)]
    pallas_call x0 -> x2, Pallas kernels: none -> 163 us  [the longest x1 82.8 us: pool_backward(): pl.pallas_call(functools.partial(backward_kernel, channels=channels), gri...]
    psum x2, waiting for transfers between devices: 63.6 us -> 188 us  [the longest x1 112 us: on_device(): lax.psum((grad_weight_one, small_grads[1].astype(BF)), 'roi')]
  transfers between devices with their start and end apart: 2 -> 3, of which waited for: 1 -> 3; matrix products, arithmetic and copies ran while one was open for 42% -> 7% of each run, Pallas kernels for 0% -> 15%
where the time goes in v1:
time: 543 us; the launch traced here: 538 us
  waiting for transfers between devices  208 us (38%)
  Pallas kernels  163 us (30%)
  blocking collectives  57.4 us (11%)
  matrix products  55.8 us (10%)
  other arithmetic  28.6 us (5%)
  between operations  15.6 us (3%)
  local copies, waits for them, and re-layouts  7.46 us (1%)
    psum x1, waiting for transfers between devices, on_device(): lax.psum((grad_weight_one, small_grads[1].astype(BF)), 'roi')  112 us
    pallas_call x1, Pallas kernels, pool_backward(): pl.pallas_call(functools.partial(backward_kernel, channels=channels), gri...  82.8 us
    pallas_call x1, Pallas kernels, pool_forward(): pl.pallas_call(functools.partial(forward_kernel, channels=channels), grid...  80.4 us
    psum x1, waiting for transfers between devices, on_device(): small = lax.psum(small_grads[0:1] + small_grads[2:], 'roi')  75.9 us
    psum x1, blocking collectives, on_device(): small = lax.psum(small_grads[0:1] + small_grads[2:], 'roi')  57.4 us
    ppermute x1, waiting for transfers between devices, on_device(): other = lax.ppermute(partial, 'ch', [(0, 1), (1, 0)])  20.6 us
    convert_element_type x1, other arithmetic, on_device(): grad_weight_one.astype(F32)  14.7 us
    dot_general x1, matrix products, on_device(): lax.dot_general(first_weight, grad_pre_one, (((1,), (1,)), ((), ())), pre...  13.5 us
  transfers between devices with their start and end apart: 3, of which 3 were waited for; matrix products, arithmetic and copies ran while one was open for 7% of the time, Pallas kernels for 15%

profile of v1, /device:TPU:4, one launch (start us, length us, event | category | flops | bytes accessed | tf_op | source)
XLA Modules:
  0.0 538.1 jit_solution(17590040613780539263)
XLA Ops:
  7.2 0.0 copy-start
  7.2 0.0 all-reduce.7.cloned.1.call-start
  7.2 0.8 convert_element_type.112
  8.1 0.7 convert_element_type.114
  8.8 1.5 copy.32
  10.2 0.7 subtract_convert_fusion
  10.9 2.0 concatenate.3.table_ref
  12.9 80.4 %pool_forward.1 = (bf16[6272,512]{1,0:T(8,128)(2,1)}, f32[24,512]{1,0:T(8,128)}) custom-call(f32[16,512]{1,0:T(8,128)} %concatenate.3.table_ref, bf16[256,4096]{1,0:T(8,128)(2,1)} %bitcast.74, bf16[256,1024]{1,0:T(8,128)(2,1)} %bitcast.75, bf16[256,256]{1,0:T(8,128)(2,1)} %bitcast.77, bf16[256,64]{1,0:T(8,128)(2,1)} %bitcast.76), custom_call_target="tpu_custom_call" | custom-call | tf_op jit(solution)/shard_map/pool_forward/pallas_call | solution.py:143
  93.3 0.0 copy-start.7
  93.3 0.0 copy-start.5
  93.3 0.0 copy-start.6
  93.3 0.0 copy-start.8
  93.3 12.1 %convolution_convert_fusion.3 = bf16[512,1024]{1,0:T(8,128)(2,1)S(1)} fusion(bf16[6272,512]{1,0:T(8,128)(2,1)} %get-tuple-element.21, bf16[6272,1024]{1,0:T(8,128)(2,1)} %param.26), kind=kOutput, calls=%fused_computation.41 | convolution fusion | flops 6577192960 | bytes 20316160 | tf_op jit(solution)/shard_map/dot_general | solution.py:379
  105.3 1.6 collective-permute-start
  106.9 0.0 copy-done.7
  106.9 0.0 copy-done.5
  106.9 0.0 copy-done.6
  106.9 0.0 copy-done.8
  106.9 20.6 %collective-permute-done = bf16[512,1024]{1,0:T(8,128)(2,1)S(1)} collective-permute-done((bf16[512,1024]{1,0:T(8,128)(2,1)S(1)}, bf16[512,1024]{1,0:T(8,128)(2,1)S(1)}, u32[]{:S(2)}, u32[]{:S(2)}) %collective-permute-start) | collective-permute-done | bytes 1048608 | tf_op jit(solution)/shard_map/ppermute | solution.py:384
  127.5 4.8 multiply_convert_fusion.1
  132.4 0.0 copy-done
  132.4 0.0 copy-start.4
  132.4 0.0 copy-start.3
  132.4 12.1 %multiply_convert_fusion = (bf16[512,1024]{1,0:T(8,128)(2,1)S(1)}, f32[512,1024]{1,0:T(8,128)S(1)}, f32[512,1024]{1,0:T(8,128)S(1)}) fusion(f32[1024]{0:T(1024)S(1)} %convert_element_type.121, bf16[512,1024]{1,0:T(8,128)(2,1)S(1)} %get-tuple-element.67, bf16[1024,1024]{1,0:T(8,128)(2,1)S(1)} %copy-done), kind=kOutput, calls=%fused_computation.11 | convolution fusion | flops 1108344832 | bytes 8392704 | tf_op jit(solution)/shard_map/dot_general | solution.py:282
  144.6 0.0 copy-done.4
  144.6 0.4 convolution_add_fusion.1
  144.9 0.9 fusion.41
  145.9 1.4 convert_reduce_fusion.3
  147.2 0.0 copy-done.3
  147.3 0.5 fusion.49
  147.7 0.1 fusion.15
  147.8 0.2 convert_reduce_fusion.2
  148.0 0.5 fusion.50
  148.4 1.3 convert_reduce_fusion
  149.7 0.0 slice-start
  149.8 1.3 fusion.51
  151.1 0.0 slice-start.1
  151.1 2.6 convolution_convert_fusion.2
  153.7 1.3 convert_reduce_fusion.1
  155.0 0.0 slice-done
  155.0 0.0 slice-done.1
  155.0 9.8 %convolution_convert_fusion = bf16[6272,1024]{1,0:T(8,128)(2,1)} fusion(bf16[6272,512]{1,0:T(8,128)(2,1)S(1)} %bitcast.87, bf16[512,1024]{1,0:T(8,128)(2,1)S(1)} %get-tuple-element.64), kind=kOutput, calls=%fused_computation | convolution fusion | flops 6583091200 | bytes 20316160 | tf_op jit(solution)/shard_map/dot_general | solution.py:402
  164.8 0.0 all-reduce.7.cloned.1.call-update
  164.8 0.0 all-reduce.5.cloned.1.call-start
  164.9 0.2 fusion.53
  165.1 1.1 fusion.52
  166.2 13.5 %fusion.gp_ref = bf16[6272,512]{1,0:T(8,128)(2,1)} fusion(bf16[512,1024]{1,0:T(8,128)(2,1)S(1)} %get-tuple-element.64, bf16[6272,1024]{1,0:T(8,128)(2,1)} %param.26), kind=kOutput, calls=%fused_computation.2 | convolution fusion | flops 6579879936 | bytes 20316160 | tf_op jit(solution)/shard_map/dot_general | solution.py:405
  179.7 0.0 all-reduce.5.cloned.1.call-update
  179.7 0.5 fusion.13
  180.2 0.6 subtract_reduce_fusion
  182.1 57.4 %all-reduce = (f32[]{:T(128)}, f32[]{:T(128)}, f32[1024]{0:T(1024)}, f32[1024]{0:T(1024)}, f32[81]{0:T(128)}, /*index=5*/f32[1024,4]{0,1:T(4,128)}, f32[4]{0:T(128)}) all-reduce(f32[]{:T(128)S(6)} %div.42, f32[]{:T(128)S(6)} %div.43, f32[1024]{0:T(1024)S(1)} %get-tuple-element.63, ...), channel_id=1, replica_groups=mesh['roi'=16,'ch'=2] {'roi'}, use_global_device_ids=true, to_apply=%region_4.5 | all-reduce | flops 6231 | bytes 49848 | tf_op jit(solution)/shard_map/psum | solution.py:409
  239.5 82.8 %pool_backward.1 = (f32[256,4096]{1,0:T(8,128)}, f32[256,1024]{1,0:T(8,128)}, f32[256,256]{1,0:T(8,128)}, f32[256,64]{1,0:T(8,128)}) custom-call(f32[24,512]{1,0:T(8,128)} %get-tuple-element.22.sorted_ref, bf16[6272,512]{1,0:T(8,128)(2,1)} %fusion.gp_ref), custom_call_target="tpu_custom_call" | custom-call | tf_op jit(solution)/shard_map/pool_backward/pallas_call | solution.py:209
  322.3 1.6 copy.34
  323.9 0.6 constant_dynamic-slice_fusion
  324.5 112.0 %all-reduce.7.cloned.1.call-done = (bf16[6272,1024]{1,0:T(8,128)(2,1)}, bf16[1024,1024]{1,0:T(8,128)(2,1)}) async-done(((bf16[6272,1024]{1,0:T(8,128)(2,1)}, bf16[1024,1024]{1,0:T(8,128)(2,1)}), (bf16[6272,1024]{1,0:T(8,128)(2,1)}, bf16[1024,1024]{1,0:T(8,128)(2,1)})) %all-reduce.7.cloned.1.call-update) | async-done | bytes 14942224 | tf_op jit(solution)/shard_map/psum | solution.py:408
  436.5 0.0 copy-start.2
  436.5 14.7 %convert_element_type.134 = f32[6272,1024]{1,0:T(8,128)} convert(bf16[6272,1024]{1,0:T(8,128)(2,1)} %get-tuple-element.51) | non-fusion elementwise | flops 6422528 | bytes 38535168 | tf_op jit(solution)/shard_map/convert_element_type | solution.py:423
  451.2 0.0 copy-start.1
  451.2 0.0 copy-done.2
  451.2 2.5 convert_element_type.137
  453.7 75.9 %all-reduce.5.cloned.1.call-done = f32[1024,81]{0,1:T(8,128)} async-done(((f32[1024,81]{0,1:T(8,128)}), f32[1024,81]{0,1:T(8,128)}) %all-reduce.5.cloned.1.call-update) | async-done | bytes 331792 | tf_op jit(solution)/shard_map/psum | solution.py:409
  529.6 1.7 copy.39
  531.3 0.0 copy-done.1
  (9 shorter events, 0.0 us)
Async XLA Ops:
  7.2 125.2 %copy-start = (bf16[1024,1024]{1,0:T(8,128)(2,1)S(1)}, bf16[1024,1024]{1,0:T(8,128)(2,1)}, u32[]{:S(2)}) copy-start(bf16[1024,1024]{1,0:T(8,128)(2,1)} %param.28) | copy-start | bytes 6291460
  7.2 429.3 %all-reduce.7.cloned.1.call-start = ((), (), s32[]{:S(2)}) async-start(), calls=%async_computation.1 | async-start | bytes 29884416 | tf_op jit(solution)/shard_map/psum | solution.py:408
  93.3 13.6 %copy-start.7 = (bf16[81]{0:T(256)(128)(2,1)S(1)}, bf16[81]{0:T(256)(128)(2,1)}, u32[]{:S(2)}) copy-start(bf16[81]{0:T(256)(128)(2,1)} %param.31) | copy-start | bytes 490
  93.3 13.6 %copy-start.5 = (bf16[1024]{0:T(1024)(128)(2,1)S(1)}, bf16[1024]{0:T(1024)(128)(2,1)}, u32[]{:S(2)}) copy-start(bf16[1024]{0:T(1024)(128)(2,1)} %param.29) | copy-start | bytes 6148
  93.3 13.6 %copy-start.6 = (bf16[1024]{0:T(1024)(128)(2,1)S(1)}, bf16[1024]{0:T(1024)(128)(2,1)}, u32[]{:S(2)}) copy-start(bf16[1024]{0:T(1024)(128)(2,1)} %param.27) | copy-start | bytes 6148
  93.3 13.7 %copy-start.8 = (bf16[4]{0:T(256)(128)(2,1)S(1)}, bf16[4]{0:T(256)(128)(2,1)}, u32[]{:S(2)}) copy-start(bf16[4]{0:T(256)(128)(2,1)} %param.33) | copy-start | bytes 28
  105.3 22.2 %collective-permute-start = (bf16[512,1024]{1,0:T(8,128)(2,1)S(1)}, bf16[512,1024]{1,0:T(8,128)(2,1)S(1)}, u32[]{:S(2)}, u32[]{:S(2)}) collective-permute-start(bf16[512,1024]{1,0:T(8,128)(2,1)S(1)} %convolution_convert_fusion.3), channel_id=1, source_target_pairs={{0,1},{1,0},{2,3},{3,2},{4,5},{5,4},{6,7},{7,6},{8,9},{9,8},{10,11... | collective-permute-start | bytes 3145736 | tf_op jit(solution)/shard_map/ppermute | solution.py:384
  132.4 12.2 %copy-start.4 = (bf16[1024,4]{0,1:T(4,128)(2,1)S(1)}, bf16[1024,4]{0,1:T(4,128)(2,1)}, u32[]{:S(2)}) copy-start(bf16[1024,4]{0,1:T(4,128)(2,1)} %param.32) | copy-start | bytes 24580
  132.4 14.8 %copy-start.3 = (bf16[1024,81]{0,1:T(8,128)(2,1)S(1)}, bf16[1024,81]{0,1:T(8,128)(2,1)}, u32[]{:S(2)}) copy-start(bf16[1024,81]{0,1:T(8,128)(2,1)} %param.30) | copy-start | bytes 497668
  149.7 5.2 slice-start
  151.1 3.9 slice-start.1
  164.8 364.7 %all-reduce.5.cloned.1.call-start = ((), (), s32[]{:S(2)}) async-start(), calls=%async_computation | async-start | bytes 720896 | tf_op jit(solution)/shard_map/psum | solution.py:409
  436.5 14.7 %copy-start.2 = (bf16[1024,1024]{1,0:T(8,128)(2,1)S(1)}, bf16[1024,1024]{1,0:T(8,128)(2,1)}, u32[]{:S(2)}) copy-start(bf16[1024,1024]{1,0:T(8,128)(2,1)} %get-tuple-element.52) | copy-start | bytes 6291460
  451.2 80.1 %copy-start.1 = (bf16[1024,1024]{1,0:T(8,128)(2,1)S(1)}, bf16[1024,1024]{1,0:T(8,128)(2,1)}, u32[]{:S(2)}) copy-start(bf16[1024,1024]{1,0:T(8,128)(2,1)} %param.28) | copy-start | bytes 6291460
Sparse Core Ops, SparseCore 0:
  164.9 271.5 all-reduce.6
  440.4 89.0 all-reduce.4

commit v2 on v1

v2 whole, which is shorter than its diff:
```python
import functools
import jax, jax.numpy as jnp
from jax import lax
from jax.sharding import PartitionSpec as P
from jax.experimental import pallas as pl
from jax.experimental.pallas import tpu as pltpu

POOL = 7
SAMPLES = 2
SIDE = 64
LANES = 128
BF = jnp.bfloat16
F32 = jnp.float32
VM = 60 * 2**20


def spread(low, high, extent):
    anchor = low * extent - 0.5
    stride = (high - low) * extent / POOL
    places = lax.broadcasted_iota(jnp.int32, (extent, LANES), 0).astype(F32)
    out = []
    for col in range(POOL):
        total = None
        for s in range(SAMPLES):
            at = jnp.clip(anchor + (col + (s + 0.5) / SAMPLES) * stride, 0.0, extent - 1.0)
            term = jnp.maximum(0.0, 1.0 - jnp.abs(at - places))
            total = term if total is None else total + term
        out.append(total / SAMPLES)
    return out


def write_tables(across_ref, down_ref, rows, extent, level):
    x1, y1, x2, y2 = (rows[k : k + 1] for k in range(4, 8))
    mask = (rows[9:10] == float(level)).astype(F32)
    across = spread(x1, x2, extent)
    down = spread(y1, y2, extent)
    for j in range(POOL):
        a = (across[j] * mask).astype(BF).astype(F32)
        if extent < 16:
            a = jnp.concatenate([a] * (16 // extent), 0)
        across_ref[j, :, :] = a.astype(BF)
    for i in range(POOL):
        d = down[i]
        if extent < 16:
            half = lax.broadcasted_iota(jnp.int32, (16, LANES), 0) < extent
            for q in range(extent // 2):
                top = jnp.broadcast_to(d[2 * q : 2 * q + 1], (16, LANES))
                low = jnp.broadcast_to(d[2 * q + 1 : 2 * q + 2], (16, LANES))
                down_ref[i, q] = jnp.where(half, top, low).astype(BF)
        else:
            for h in range(extent):
                down_ref[i, h] = jnp.broadcast_to(d[h : h + 1], (16, LANES)).astype(BF)


def kernel_row(k_ref, across_ref, down_ref, i, extent):
    wide = max(extent, 16)
    tiles = extent * extent // wide
    down = down_ref[i, 0:tiles].reshape(tiles, 1, 16, LANES)
    for j in range(POOL):
        across = across_ref[j, 0:wide, :].reshape(1, wide // 16, 16, LANES)
        k_ref[0 : extent * extent, j * LANES : (j + 1) * LANES] = (across * down).reshape(
            extent * extent, LANES
        )


def over_rows(k_refs, make, use):
    first, second = k_refs
    make(first, 0)

    def pair(p, c):
        make(second, 2 * p + 1)
        use(first, 2 * p)
        make(first, 2 * p + 2)
        use(second, 2 * p + 1)
        return c

    lax.fori_loop(0, POOL // 2, pair, 0)
    use(first, POOL - 1)


def sort_tables(table):
    n = table.shape[1]
    level = table[9:10]
    which = lax.broadcasted_iota(jnp.int32, (8, n), 0).astype(F32)
    onehot = (level == which).astype(F32)
    before = (
        lax.broadcasted_iota(jnp.int32, (n, n), 0) < lax.broadcasted_iota(jnp.int32, (n, n), 1)
    ).astype(BF)
    earlier = jnp.dot(onehot.astype(BF), before, preferred_element_type=F32)
    lower = (which < level).astype(F32) * 1.0
    counts = jnp.sum(onehot, axis=1, keepdims=True)
    rank = jnp.sum(onehot * earlier + lower * counts, axis=0, keepdims=True)
    return rank


def permute(table, rank):
    n = table.shape[1]
    place = lax.broadcasted_iota(jnp.int32, (n, n), 0).astype(F32)
    q = (rank == place).astype(F32)
    return lax.dot_general(
        table, q, (((1,), (1,)), ((), ())), precision=lax.Precision.HIGHEST, preferred_element_type=F32
    )


def forward_kernel(base_ref, boxes_ref, targets_ref, image_ref, level_ref, label_ref, p2, p3, p4, p5, out_ref, sorted_ref, acc, acr, dwn, kone, ktwo, *, channels):
    pyr = (p2, p3, p4, p5)
    tile = pl.program_id(0)

    @pl.when(tile == 0)
    def _():
        count = boxes_ref.shape[1]
        table = jnp.concatenate(
            [
                targets_ref[...],
                boxes_ref[...],
                (image_ref[...] - base_ref[0]).astype(F32),
                level_ref[...].astype(F32),
                label_ref[...].astype(F32),
                jnp.zeros((5, count), F32),
            ]
        )
        rank = sort_tables(table)
        full = permute(table, rank)
        sorted_ref[0:16, :] = full
        sorted_ref[16:24, :] = jnp.broadcast_to(rank, (8, count))

    rows = sorted_ref[0:16, pl.ds(pl.multiple_of(tile * LANES, LANES), LANES)]
    acc[...] = jnp.zeros_like(acc)
    first = rows[8:9] == 0.0
    cells = POOL * POOL
    for level in range(4):
        extent = SIDE // 2**level
        size = extent * extent
        here = jnp.sum((rows[9:10] == float(level)).astype(F32)) > 0.0

        @pl.when(here)
        def _():
            wide = max(extent, 16)
            a_ref = acr.at[:, 0:wide, :]
            write_tables(a_ref, dwn, rows, extent, level)

            def make(k_ref, i):
                kernel_row(k_ref, a_ref, dwn, i, extent)

            def use(k_ref, i):
                got = jnp.dot(pyr[level][...], k_ref[0:size, :], preferred_element_type=F32)
                sel = jnp.where(
                    jnp.concatenate([first] * POOL, 1), got[:channels], got[channels:]
                )
                for j in range(POOL):
                    at = pl.ds(i * POOL + j, channels, stride=cells)
                    acc[at, :] = acc[at, :] + sel[:, j * LANES : (j + 1) * LANES]

            over_rows((kone, ktwo), make, use)

    out_ref[...] = acc[...].astype(BF)


def pool_forward(base, boxes, targets, image, level, label, maps, channels):
    n = boxes.shape[1]
    rows = (boxes, targets, image, level, label)
    flat = channels * POOL * POOL
    full = lambda a: pl.BlockSpec(a.shape, lambda t: (0,) * a.ndim)
    return pl.pallas_call(
        functools.partial(forward_kernel, channels=channels),
        grid=(n // LANES,),
        in_specs=[pl.BlockSpec(memory_space=pltpu.SMEM)] + [full(a) for a in rows] + [full(m) for m in maps],
        out_specs=[
            pl.BlockSpec((flat, LANES), lambda t: (0, t)),
            pl.BlockSpec((24, n), lambda t: (0, 0)),
        ],
        out_shape=[
            jax.ShapeDtypeStruct((flat, n), BF),
            jax.ShapeDtypeStruct((24, n), F32),
        ],
        scratch_shapes=[
            pltpu.VMEM((flat, LANES), F32),
            pltpu.VMEM((POOL, SIDE, LANES), BF),
            pltpu.VMEM((POOL, SIDE, 16, LANES), BF),
            pltpu.VMEM((SIDE * SIDE, POOL * LANES), BF),
            pltpu.VMEM((SIDE * SIDE, POOL * LANES), BF),
        ],
        compiler_params=pltpu.CompilerParams(vmem_limit_bytes=VM),
        cost_estimate=pl.CostEstimate(flops=40 * 10**9, bytes_accessed=10**7, transcendentals=0),
        name="pool_forward",
    )(base, *rows, *maps)


def backward_kernel(sorted_ref, gp_ref, o2, o3, o4, o5, g32, acr, dwn, kone, ktwo, gbuf, *, channels):
    outs = (o2, o3, o4, o5)
    tile = pl.program_id(0)

    @pl.when(tile == 0)
    def _():
        for o in outs:
            o[...] = jnp.zeros_like(o)

    rows = sorted_ref[0:16, pl.ds(pl.multiple_of(tile * LANES, LANES), LANES)]
    g32[...] = gp_ref[...].astype(F32) * (1.0 / 3.0)
    first = rows[8:9] == 0.0
    cells = POOL * POOL
    for level in range(4):
        extent = SIDE // 2**level
        size = extent * extent
        here = jnp.sum((rows[9:10] == float(level)).astype(F32)) > 0.0

        @pl.when(here)
        def _():
            wide = max(extent, 16)
            a_ref = acr.at[:, 0:wide, :]
            write_tables(a_ref, dwn, rows, extent, level)

            def make(k_ref, i):
                kernel_row(k_ref, a_ref, dwn, i, extent)

            def use(k_ref, i):
                for j in range(POOL):
                    g = g32[pl.ds(i * POOL + j, channels, stride=cells), :]
                    gbuf[0:channels, j * LANES : (j + 1) * LANES] = jnp.where(first, g, 0.0).astype(BF)
                    gbuf[channels:, j * LANES : (j + 1) * LANES] = jnp.where(first, 0.0, g).astype(BF)
                outs[level][...] += lax.dot_general(
                    gbuf[...], k_ref[0:size, :], (((1,), (1,)), ((), ())), preferred_element_type=F32
                )

            over_rows((kone, ktwo), make, use)


def pool_backward(sorted_table, gp, channels):
    n = sorted_table.shape[1]
    flat = channels * POOL * POOL
    sizes = [(SIDE // 2**l) ** 2 for l in range(4)]
    return pl.pallas_call(
        functools.partial(backward_kernel, channels=channels),
        grid=(n // LANES,),
        in_specs=[
            pl.BlockSpec(sorted_table.shape, lambda t: (0, 0)),
            pl.BlockSpec((flat, LANES), lambda t: (0, t)),
        ],
        out_specs=[pl.BlockSpec((2 * channels, s), lambda t: (0, 0)) for s in sizes],
        out_shape=[jax.ShapeDtypeStruct((2 * channels, s), F32) for s in sizes],
        scratch_shapes=[
            pltpu.VMEM((flat, LANES), F32),
            pltpu.VMEM((POOL, SIDE, LANES), BF),
            pltpu.VMEM((POOL, SIDE, 16, LANES), BF),
            pltpu.VMEM((SIDE * SIDE, POOL * LANES), BF),
            pltpu.VMEM((SIDE * SIDE, POOL * LANES), BF),
            pltpu.VMEM((2 * channels, POOL * LANES), BF),
        ],
        compiler_params=pltpu.CompilerParams(vmem_limit_bytes=VM),
        cost_estimate=pl.CostEstimate(flops=40 * 10**9, bytes_accessed=10**7, transcendentals=0),
        name="pool_backward",
    )(sorted_table, gp)


BOX = 96
ROOT = 0.7071067811865476
DENSITY = 0.3989422804014327
STRIP = 16


def unit_and_slope(x):
    below = 0.5 + 0.5 * lax.erf(x * ROOT)
    return x * below, below + x * jnp.exp(-0.5 * x * x) * DENSITY


def strips(rows, work, carry):
    def step(k, c):
        return work(pl.ds(pl.multiple_of(k * STRIP, STRIP), STRIP), c)

    return lax.fori_loop(0, rows // STRIP, step, carry)


def head_kernel(
    part_ref,
    ordered_ref,
    own_ref,
    other_ref,
    bias_one,
    weight_two,
    bias_two,
    weight_out,
    bias_out,
    grad_one,
    grad_two_weight,
    small,
    last,
    decoded_ref,
    act_one,
    act_two,
    grad_two,
    slope_one,
    slope_two,
    wide,
    *,
    classes,
    norm,
):
    rows, hidden = own_ref.shape
    lanes = weight_out.shape[1]

    def one(at, c):
        x = own_ref[at, :].astype(F32) + other_ref[at, :].astype(F32) + bias_one[...]
        act, slope = unit_and_slope(x)
        act_one[at, :] = act.astype(BF)
        slope_one[at, :] = slope
        return c

    strips(rows, one, 0)
    wide[...] = jnp.dot(act_one[...], weight_two[...], preferred_element_type=F32)

    def two(at, c):
        act, slope = unit_and_slope(wide[at, :] + bias_two[...])
        act_two[at, :] = act.astype(BF)
        slope_two[at, :] = slope
        return c

    strips(rows, two, 0)
    out = jnp.dot(act_two[...], weight_out[...], preferred_element_type=F32) + bias_out[...]
    ordered = ordered_ref[...]
    aux = jnp.concatenate(
        [
            jnp.zeros((BOX - 8, rows), F32),
            ordered[8:16],
            ordered[0:8],
            jnp.zeros((lanes - BOX - 8, rows), F32),
        ]
    ).T
    lane = lax.broadcasted_iota(jnp.int32, (rows, lanes), 1)
    is_class = lane < classes
    is_box = (lane >= BOX) & (lane < BOX + 4)
    label = aux[:, BOX - 6 : BOX - 5]
    hit = (lane.astype(F32) == label).astype(F32)
    fore = (label < classes - 1.0).astype(F32)
    scores = jnp.where(is_class, out, -3.0e38)
    top = jnp.max(scores, axis=1, keepdims=True)
    powers = jnp.where(is_class, jnp.exp(scores - top), 0.0)
    total = jnp.sum(powers, axis=1, keepdims=True)
    chosen = jnp.sum(jnp.where(is_class, out * hit, 0.0), axis=1, keepdims=True)
    class_loss = jnp.sum(top + jnp.log(total) - chosen, axis=0, keepdims=True) / norm
    residue = out - aux
    size = jnp.abs(residue)
    huber = jnp.where(size < 1.0, 0.5 * residue * residue, size - 0.5)
    huber = jnp.sum(jnp.where(is_box, huber, 0.0), axis=1, keepdims=True) * fore
    box_loss = jnp.sum(huber, axis=0, keepdims=True) / norm
    grad_out = jnp.where(
        is_class,
        (powers / total - hit) / norm,
        jnp.where(is_box, fore * jnp.clip(residue, -1.0, 1.0) / norm, 0.0),
    ).astype(BF)
    bias_sums = jnp.sum(grad_out.astype(F32), axis=0, keepdims=True)
    last[...] = jnp.concatenate(
        [
            bias_sums,
            jnp.broadcast_to(class_loss, (1, lanes)),
            jnp.broadcast_to(box_loss, (1, lanes)),
            jnp.zeros((5, lanes), F32),
        ]
    )
    moves = out.T[BOX : BOX + 4]
    x1, y1, x2, y2 = (ordered[k : k + 1] for k in range(4, 8))
    width, height = x2 - x1, y2 - y1
    px = moves[0:1] / 10.0 * width + (x1 + 0.5 * width)
    py = moves[1:2] / 10.0 * height + (y1 + 0.5 * height)
    half_w = 0.5 * (jnp.exp(moves[2:3] / 5.0) * width)
    half_h = 0.5 * (jnp.exp(moves[3:4] / 5.0) * height)
    boxes = jnp.concatenate(
        [px - half_w, py - half_h, px + half_w, py + half_h, jnp.zeros((4, rows), F32)]
    )
    place = lax.broadcasted_iota(jnp.int32, (rows, rows), 0).astype(F32)
    back = (ordered_ref[16:17, :] == place).astype(F32)
    decoded_ref[...] = jnp.dot(
        boxes, back, precision=lax.Precision.HIGHEST, preferred_element_type=F32
    )
    wide[...] = lax.dot_general(
        grad_out, weight_out[...], (((1,), (1,)), ((), ())), preferred_element_type=F32
    )

    def three(at, c):
        g = (wide[at, :] * slope_two[at, :]).astype(BF)
        grad_two[at, :] = g
        g = g.astype(F32)
        return c + g[0:8] + g[8:16]

    bias_two_sum = strips(rows, three, jnp.zeros((8, hidden), F32))
    wide[...] = lax.dot_general(
        grad_two[...], weight_two[...], (((1,), (1,)), ((), ())), preferred_element_type=F32
    )

    def four(at, c):
        g = (wide[at, :] * slope_one[at, :]).astype(BF)
        grad_one[at, :] = g
        g = g.astype(F32)
        return c + g[0:8] + g[8:16]

    bias_one_sum = strips(rows, four, jnp.zeros((8, hidden), F32))
    part = grad_two_weight.shape[0]
    columns = pl.ds(pl.multiple_of(part_ref[0] * part, part), part)
    grad_two_weight[...] = lax.dot_general(
        act_one[:, columns], grad_two[...], (((0,), (0,)), ((), ())), preferred_element_type=F32
    ).astype(BF)
    products = lax.dot_general(
        grad_out, act_two[...], (((0,), (0,)), ((), ())), preferred_element_type=F32
    )
    sums = jnp.concatenate(
        [
            jnp.sum(bias_one_sum, axis=0, keepdims=True),
            jnp.sum(bias_two_sum, axis=0, keepdims=True),
            jnp.zeros((lanes - BOX - 10, hidden), F32),
        ]
    )
    small[...] = jnp.concatenate([products[: BOX + 8], sums]).astype(BF)


def head_pass(
    part, parts, ordered, own, other, bias_one, weight_two, bias_two, weight_out, bias_out, classes, norm
):
    rows, hidden = own.shape
    lanes = weight_out.shape[1]
    whole = pl.BlockSpec(memory_space=pltpu.VMEM)
    return pl.pallas_call(
        functools.partial(head_kernel, classes=classes, norm=norm),
        in_specs=[pl.BlockSpec(memory_space=pltpu.SMEM)] + [whole] * 8,
        out_specs=[whole] * 5,
        out_shape=[
            jax.ShapeDtypeStruct((rows, hidden), BF),
            jax.ShapeDtypeStruct((hidden // parts, hidden), BF),
            jax.ShapeDtypeStruct((lanes, hidden), BF),
            jax.ShapeDtypeStruct((8, lanes), F32),
            jax.ShapeDtypeStruct((8, rows), F32),
        ],
        scratch_shapes=[pltpu.VMEM((rows, hidden), BF)] * 3 + [pltpu.VMEM((rows, hidden), F32)] * 3,
        compiler_params=pltpu.CompilerParams(vmem_limit_bytes=VM),
        cost_estimate=pl.CostEstimate(
            flops=6 * rows * hidden * hidden, bytes_accessed=8 * rows * hidden, transcendentals=0
        ),
        name="head",
    )(part, ordered, own, other, bias_one, weight_two, bias_two, weight_out, bias_out)


def partners(stride):
    return [(k, k ^ stride) for k in range(lax.axis_size("roi"))]


def halve(sums, axis, stride, size):
    while size > 1:
        mine = (lax.axis_index("roi") // stride) % 2
        shape = sums.shape
        split = sums.reshape(shape[:axis] + (size // 2, 2) + shape[axis + 1 :])
        keep = lax.dynamic_index_in_dim(split, mine, axis + 1, False)
        send = lax.dynamic_index_in_dim(split, 1 - mine, axis + 1, False)
        come = lax.ppermute(send, "roi", partners(stride))
        sums = (keep.astype(F32) + come.astype(F32)).astype(BF)
        stride, size = 2 * stride, size // 2
    return lax.squeeze(sums, (axis,))


def add_up_everywhere(values):
    stride = 1
    while stride < lax.axis_size("roi"):
        values = values + lax.ppermute(values, "roi", partners(stride))
        stride *= 2
    return values


def row_parts(rows):
    unit = 8 if rows % 8 == 0 else 1
    units = rows // unit
    last = max(1, units // 4)
    first = (units - last) // 2
    return (first * unit, (units - last - first) * unit, last * unit)


def spread_out(mine):
    stride, axis, shape = lax.axis_size("roi") // 2, 0, mine.shape
    while stride:
        low = (lax.axis_index("roi") // stride) % 2 == 0
        come = lax.ppermute(mine, "roi", partners(stride))
        mine = jnp.stack([jnp.where(low, mine, come), jnp.where(low, come, mine)], axis)
        stride, axis = stride // 2, axis + 1
    return mine.reshape(-1, shape[-1])


def on_device(
    pyramid_two,
    pyramid_three,
    pyramid_four,
    pyramid_five,
    proposals,
    image_index,
    levels,
    labels,
    targets,
    first_weight,
    first_bias,
    second_weight,
    second_bias,
    class_weight,
    class_bias,
    box_weight,
    box_bias,
):
    features = (pyramid_two, pyramid_three, pyramid_four, pyramid_five)
    images_here, channels_here = (pyramid_two.shape[0], pyramid_two.shape[1])
    regions_here = proposals.shape[1]
    ways, groups = lax.axis_size("roi"), lax.axis_size("ch")
    outer, inner = 4, ways // 8
    flat, hidden = first_weight.shape
    classes = class_weight.shape[1]
    share = flat // ways
    core = lax.axis_index("roi") % 2
    group = lax.axis_index("ch")
    maps = [f.reshape(images_here * channels_here, -1) for f in features]
    base = jnp.reshape(lax.axis_index("roi") * images_here, (1,)).astype(jnp.int32)
    pooled, ordered = pool_forward(
        base, proposals, targets, image_index[None], levels[None], labels[None], maps, channels_here
    )
    partial = lax.dot_general(
        pooled, first_weight, (((0,), (0,)), ((), ())), preferred_element_type=F32
    )
    if groups == 2:
        partial = partial.astype(BF)
        other = lax.ppermute(partial, "ch", [(0, 1), (1, 0)])
    else:
        partial = lax.psum(partial, "ch")
        other = jnp.zeros(partial.shape, BF)
    by_core = pooled.reshape(ways // 2, 2, share, regions_here)
    mine = lax.dynamic_index_in_dim(by_core, core, 1, False)
    theirs = lax.ppermute(lax.dynamic_index_in_dim(by_core, 1 - core, 1, False), "roi", partners(1))
    both = jnp.concatenate([mine, theirs], 2)
    gap = jnp.zeros((hidden, BOX - classes), BF)
    tail = jnp.zeros((hidden, 128 - BOX - 4), BF)
    weight_out = jnp.concatenate([class_weight, gap, box_weight, tail], 1)
    bias_out = jnp.concatenate([class_bias, gap[0], box_bias, tail[0]]).astype(F32)[None]
    grad_pre_one, grad_two, small, last, decoded = head_pass(
        jnp.reshape(group, (1,)).astype(jnp.int32),
        groups,
        ordered,
        partial,
        other,
        first_bias.astype(F32)[None],
        second_weight,
        second_bias.astype(F32)[None],
        weight_out,
        bias_out,
        classes,
        float(regions_here * ways),
    )
    grad_both = jnp.concatenate([grad_pre_one, lax.ppermute(grad_pre_one, "roi", partners(1))], 0)
    extra = jnp.concatenate([grad_two, small])
    extra_share = extra.shape[0] // ways
    extra = halve(extra.reshape(ways // 2, 2, extra_share, hidden), 1, 1, 2)
    extra = extra.reshape(outer, inner, extra_share, hidden)
    parts, at = [], 0
    split = row_parts(share)
    for rows in split:
        rows_both = both[:, at : at + rows].reshape(-1, 2 * regions_here)
        part = jnp.dot(rows_both, grad_both, preferred_element_type=F32).astype(BF)
        parts.append(part.reshape(outer, inner, rows, hidden))
        at += rows
    parts[2] = jnp.concatenate([parts[2], extra], 2)
    first_sum = halve(halve(parts[0], 1, 2, inner), 0, 2 * inner, outer)
    second_sum = halve(halve(parts[1], 1, 2, inner), 0, 2 * inner, outer)
    third_sum = halve(halve(parts[2], 0, 2 * inner, outer), 0, 2, inner)
    share_sum = jnp.concatenate([first_sum, second_sum, third_sum[: split[2]]])
    grad_weight_one = lax.all_gather(share_sum, "roi", tiled=True).astype(F32)
    extra = spread_out(third_sum[split[2] :])
    part_rows = hidden // groups
    small = extra[part_rows:].astype(F32)
    if groups == 2:
        two = extra[:part_rows]
        two_other = lax.ppermute(two, "ch", [(0, 1), (1, 0)])
        two = jnp.concatenate(
            [jnp.where(group == 0, two, two_other), jnp.where(group == 0, two_other, two)]
        )
    else:
        two = lax.all_gather(extra[:part_rows], "ch", tiled=True)
    grad_pooled = lax.dot_general(
        first_weight, grad_pre_one, (((1,), (1,)), ((), ())), preferred_element_type=F32
    ).astype(BF)
    last = add_up_everywhere(last)
    share_rows = regions_here // groups
    decoded = lax.dynamic_slice(decoded, (0, group * share_rows), (4, share_rows))
    map_grads = pool_backward(ordered, grad_pooled, channels_here)
    pyramid_grads = [g.reshape(f.shape) for g, f in zip(map_grads, features)]
    return (
        last[1, 0],
        last[2, 0],
        decoded,
        grad_weight_one,
        small[BOX + 8],
        two.astype(F32),
        small[BOX + 9],
        small[:classes].T,
        last[0, :classes],
        small[BOX : BOX + 4].T,
        last[0, BOX : BOX + 4],
        pyramid_grads[0],
        pyramid_grads[1],
        pyramid_grads[2],
        pyramid_grads[3],
    )


def solution(mesh):
    return jax.shard_map(
        on_device,
        mesh=mesh,
        in_specs=(
            P("roi", "ch", None),
            P("roi", "ch", None),
            P("roi", "ch", None),
            P("roi", "ch", None),
            P(None, "roi"),
            P("roi"),
            P("roi"),
            P("roi"),
            P(None, "roi"),
            P("ch", None),
            P(),
            P(),
            P(),
            P(),
            P(),
            P(),
            P(),
        ),
        out_specs=(
            P(),
            P(),
            P(None, ("roi", "ch")),
            P("ch", None),
            P(),
            P(),
            P(),
            P(),
            P(),
            P(),
            P(),
            P("roi", "ch", None),
            P("roi", "ch", None),
            P("roi", "ch", None),
            P("roi", "ch", None),
        ),
        check_vma=False,
    )
```

time: 543 us -> 403 us (0.74)
  waiting for transfers between devices: 208 us -> 127 us
  blocking collectives: 57.4 us -> 0 us
  Pallas kernels: 163 us -> 112 us
  starting transfers between devices: 1.63 us -> 48 us
  matrix products: 55.8 us -> 32.2 us
  local copies, waits for them, and re-layouts: 7.46 us -> 26.3 us
  other arithmetic: 28.6 us -> 35.4 us
    psum x2 -> x0, waiting for transfers between devices: 188 us -> none  [the longest x1 112 us: on_device(): lax.psum((grad_weight_one, small_grads[1].astype(BF)), 'roi')]
    ppermute x0 -> x21, waiting for transfers between devices: none -> 109 us  [the longest x10 71.1 us: halve(): come = lax.ppermute(send, 'roi', partners(stride))]
    psum x1 -> x0, blocking collectives: 57.4 us -> none  [on_device(): small = lax.psum(small_grads[0:1] + small_grads[2:], 'roi')]
    ppermute x0 -> x21, starting transfers between devices: none -> 46.4 us  [the longest x4 17.7 us: add_up_everywhere(): values = values + lax.ppermute(values, 'roi', partners(stride))]
    pallas_call x1, Pallas kernels: 80.4 us -> 47 us  [pool_forward(): pl.pallas_call(functools.partial(forward_kernel, channels=channels), grid...]
    pallas_call x1, Pallas kernels: 82.8 us -> 52.2 us  [pool_backward(): pl.pallas_call(functools.partial(backward_kernel, channels=channels), gri...]
    dot_general x11 -> x3, matrix products: 30.3 us -> 7.96 us  [on_device(): part = jnp.dot(rows_both, grad_both, preferred_element_type=F32).astype(BF)]
    pallas_call x0 -> x1, Pallas kernels: none -> 12.6 us  [head_pass(): pl.pallas_call(functools.partial(head_kernel, classes=classes, norm=norm)...]
  transfers between devices with their start and end apart: 3 -> 23, of which waited for: 3 -> 11; matrix products, arithmetic and copies ran while one was open for 7% -> 16% of each run, Pallas kernels for 15% -> 16%
where the time goes in v2:
time: 403 us; the launch traced here: 396 us
  waiting for transfers between devices  127 us (32%)
  Pallas kernels  112 us (28%)
  starting transfers between devices  48 us (12%)
  other arithmetic  35.4 us (9%)
  matrix products  32.2 us (8%)
  local copies, waits for them, and re-layouts  26.3 us (7%)
  between operations  14.8 us (4%)
    ppermute x10, waiting for transfers between devices, halve(): come = lax.ppermute(send, 'roi', partners(stride))  71.1 us
    pallas_call x1, Pallas kernels, pool_backward(): pl.pallas_call(functools.partial(backward_kernel, channels=channels), gri...  52.2 us
    pallas_call x1, Pallas kernels, pool_forward(): pl.pallas_call(functools.partial(forward_kernel, channels=channels), grid...  47 us
    ppermute x1, waiting for transfers between devices, on_device(): two_other = lax.ppermute(two, 'ch', [(0, 1), (1, 0)])  21.3 us
    ppermute x1, waiting for transfers between devices, on_device(): other = lax.ppermute(partial, 'ch', [(0, 1), (1, 0)])  18.1 us
    ppermute x4, starting transfers between devices, add_up_everywhere(): values = values + lax.ppermute(values, 'roi', partners(stride))  17.7 us
    ppermute x4, waiting for transfers between devices, spread_out(): come = lax.ppermute(mine, 'roi', partners(stride))  15.5 us
    convert_element_type x1, other arithmetic, on_device(): grad_weight_one = lax.all_gather(share_sum, 'roi', tiled=True).astype(F32)  14.5 us
  transfers between devices with their start and end apart: 23, of which 11 were waited for; matrix products, arithmetic and copies ran while one was open for 16% of the time, Pallas kernels for 16%

profile of v2, /device:TPU:4, one launch (start us, length us, event | category | flops | bytes accessed | tf_op | source)
XLA Modules:
  0.0 395.8 jit_solution(17199036578800524346)
XLA Ops:
  7.2 1.5 copy.49
  8.7 47.0 %pool_forward.1 = (bf16[6272,512]{1,0:T(8,128)(2,1)}, f32[24,512]{1,0:T(8,128)}) custom-call(s32[1]{0:T(128)} %bitcast.1.base_ref, f32[4,512]{1,0:T(4,128)} %boxes_ref.1, f32[4,512]{1,0:T(4,128)} %targets_ref.1, s32[1,512]{1,0:T(1,128)} %bitcast.174, s32[1,512]{1,0:T(1,128)} %bitcast.175, s32[1,512]{1,0:T(1,128)} %bitcast.176, bf16[256,4096]{1,0:T(8,128)(2,1)} %bitcast.171, ...), custom_call_target="tpu_custom_call" | custom-call | flops 40000000000 | bytes 10000000 | tf_op jit(solution)/shard_map/pool_forward/pallas_call | solution.py:164
  55.8 5.3 %dynamic-slice_bitcast_fusion.1 = (bf16[8,392,512]{2,1,0:T(8,128)(2,1)S(1)}, bf16[8,392,512]{2,1,0:T(8,128)(2,1)}) fusion(bf16[8,2,392,512]{3,2,1,0:T(8,128)(2,1)} %bitcast.145, s32[]{:T(128)S(6)} %select_n.176, s32[]{:T(128)S(6)} %select_n.177), kind=kLoop, calls=%fused_computation.9 | loop fusion | bytes 12845064 | tf_op jit(solution)/shard_map/jit(dynamic_index_in_dim)/squeeze | solution.py:527
  61.1 12.1 %collective-permute-start.5 = (bf16[8,392,512]{2,1,0:T(8,128)(2,1)}, bf16[8,392,512]{2,1,0:T(8,128)(2,1)}, u32[]{:S(2)}, u32[]{:S(2)}) collective-permute-start(bf16[8,392,512]{2,1,0:T(8,128)(2,1)} %get-tuple-element.83), channel_id=1, source_target_pairs={{0,2},{2,0},{4,6},{6,4},{8,10},{10,8},{12,14},{14,12},{16,18},{18,... | collective-permute-start | bytes 9633800 | tf_op jit(solution)/shard_map/ppermute | solution.py:528
  73.2 10.8 %convolution_convert_fusion.4.own_ref = bf16[512,1024]{1,0:T(8,128)(2,1)} fusion(bf16[6272,512]{1,0:T(8,128)(2,1)S(1)} %copy-done, bf16[6272,1024]{1,0:T(8,128)(2,1)} %param.26), kind=kOutput, calls=%fused_computation.25 | convolution fusion | flops 6577192960 | bytes 20316160 | tf_op jit(solution)/shard_map/dot_general | solution.py:517
  84.0 1.5 collective-permute-start
  85.5 0.6 broadcast_in_dim.35
  86.1 0.6 broadcast_in_dim.36
  86.7 0.9 copy.51
  87.6 1.1 copy.50
  88.9 0.6 fusion.16.bias_out
  89.4 1.8 maximum_maximum_fusion.weight_out
  91.3 18.1 %collective-permute-done.other_ref = bf16[512,1024]{1,0:T(8,128)(2,1)} collective-permute-done((bf16[512,1024]{1,0:T(8,128)(2,1)}, bf16[512,1024]{1,0:T(8,128)(2,1)}, u32[]{:S(2)}, u32[]{:S(2)}) %collective-permute-start) | collective-permute-done | bytes 1048608 | tf_op jit(solution)/shard_map/ppermute | solution.py:522
  109.4 12.6 %head.1 = (bf16[512,1024]{1,0:T(8,128)(2,1)}, bf16[512,1024]{1,0:T(8,128)(2,1)}, bf16[128,1024]{1,0:T(8,128)(2,1)}, f32[8,128]{1,0:T(8,128)}, f32[8,512]{1,0:T(8,128)}) custom-call(s32[1]{0:T(128)} %bitcast.part_ref, f32[24,512]{1,0:T(8,128)} %get-tuple-element.26.ordered_ref.sorted_ref, bf16[512,1024]{1,0:T(8,128)(2,1)} %convolution_convert_fusion.4.own_ref, ...), custom_call_target="tpu_custom_call" | custom-call | flops 3221225472 | bytes 4194304 | tf_op jit(solution)/shard_map/head/pallas_call | solution.py:420
  122.0 1.4 pad_maximum_fusion.1
  123.5 1.0 copy-done.5
  124.5 0.9 dynamic-slice_bitcast_fusion.4
  125.9 1.4 constant_dynamic-update-slice_fusion.1
  127.3 0.7 collective-permute-done.13
  128.0 1.3 fusion.6
  129.3 1.5 constant_dynamic-update-slice_fusion
  130.9 1.3 pad_maximum_fusion
  132.2 1.8 convolution_convert_fusion.3
  134.0 1.1 copy-done.1
  135.1 1.1 fusion.10
  136.3 2.6 collective-permute-start.14
  138.9 1.6 fusion.3
  140.5 2.8 convolution_convert_fusion.2
  143.3 1.2 dynamic-slice_bitcast_fusion.3
  144.6 0.6 copy-done.9
  145.1 1.6 fusion.1
  146.8 3.4 convolution_convert_fusion.1
  150.2 1.4 copy-done.7
  151.6 1.2 dynamic-slice_bitcast_fusion.2
  152.8 2.0 collective-permute-start.10
  154.8 9.4 %collective-permute-done.14 = bf16[2,2,136,1024]{3,2,1,0:T(8,128)(2,1)} collective-permute-done((bf16[2,2,136,1024]{3,2,1,0:T(8,128)(2,1)}, bf16[2,2,136,1024]{3,2,1,0:T(8,128)(2,1)}, u32[]{:S(2)}, u32[]{:S(2)}) %collective-permute-start.14) | collective-permute-done | bytes 1114144 | tf_op jit(solution)/shard_map/ppermute | solution.py:451
  164.3 1.7 fusion.5
  166.0 2.8 collective-permute-start.15
  168.8 5.4 %collective-permute-done.7 = bf16[4,1,144,1024]{3,2,0,1:T(8,128)(2,1)} collective-permute-done((bf16[4,1,144,1024]{3,2,0,1:T(8,128)(2,1)}, bf16[4,1,144,1024]{3,2,0,1:T(8,128)(2,1)}, u32[]{:S(2)}, u32[]{:S(2)}) %collective-permute-start.7) | collective-permute-done | bytes 1179680 | tf_op jit(solution)/shard_map/ppermute | solution.py:451
  174.3 1.7 fusion.4
  176.1 23.8 %collective-permute-done.10 = bf16[4,1,152,1024]{3,2,0,1:T(8,128)(2,1)S(1)} collective-permute-done((bf16[4,1,152,1024]{3,2,0,1:T(8,128)(2,1)}, bf16[4,1,152,1024]{3,2,0,1:T(8,128)(2,1)S(1)}, u32[]{:S(2)}, u32[]{:S(2)}) %collective-permute-start.10) | collective-permute-done | bytes 1245216 | tf_op jit(solution)/shard_map/ppermute | solution.py:451
  201.8 2.8 collective-permute-start.9
  204.6 17.5 %collective-permute-done.11 = bf16[2,152,1024]{2,1,0:T(8,128)(2,1)S(1)} collective-permute-done((bf16[2,152,1024]{2,1,0:T(8,128)(2,1)S(1)}, bf16[2,152,1024]{2,1,0:T(8,128)(2,1)S(1)}, u32[]{:S(2)}, u32[]{:S(2)}) %collective-permute-start.11) | collective-permute-done | bytes 622624 | tf_op jit(solution)/shard_map/ppermute | solution.py:451
  222.4 0.6 collective-permute-start.12
  223.2 14.2 %collective-permute-done.12 = bf16[1,152,1024]{2,1,0:T(8,128)(2,1)S(1)} collective-permute-done((bf16[1,152,1024]{2,1,0:T(8,128)(2,1)S(1)}, bf16[1,152,1024]{2,1,0:T(8,128)(2,1)S(1)}, u32[]{:S(2)}, u32[]{:S(2)}) %collective-permute-start.12) | collective-permute-done | bytes 311328 | tf_op jit(solution)/shard_map/ppermute | solution.py:451
  237.5 0.9 pad_maximum_fusion.3
  238.6 6.0 %collective-permute-done.17 = bf16[40,1024]{1,0:T(8,128)(2,1)S(1)} collective-permute-done((bf16[40,1024]{1,0:T(8,128)(2,1)S(1)}, bf16[40,1024]{1,0:T(8,128)(2,1)S(1)}, u32[]{:S(2)}, u32[]{:S(2)}) %collective-permute-start.17) | collective-permute-done | bytes 81952 | tf_op jit(solution)/shard_map/ppermute | solution.py:477
  244.8 1.1 collective-permute-done.1
  245.9 0.9 collective-permute-start.2
  246.9 9.5 %collective-permute-done.18 = bf16[2,40,1024]{2,1,0:T(8,128)(2,1)S(1)} collective-permute-done((bf16[2,40,1024]{2,1,0:T(8,128)(2,1)S(1)}, bf16[2,40,1024]{2,1,0:T(8,128)(2,1)S(1)}, u32[]{:S(2)}, u32[]{:S(2)}) %collective-permute-start.18) | collective-permute-done | bytes 163872 | tf_op jit(solution)/shard_map/ppermute | solution.py:477
  256.4 2.8 collective-permute-start.19
  259.3 13.5 %fusion.gp_ref = bf16[6272,512]{1,0:T(8,128)(2,1)} fusion(bf16[512,1024]{1,0:T(8,128)(2,1)S(1)} %copy-done.11, bf16[6272,1024]{1,0:T(8,128)(2,1)} %param.26), kind=kOutput, calls=%fused_computation.1 | convolution fusion | flops 6579879936 | bytes 20316160 | tf_op jit(solution)/shard_map/dot_general | solution.py:577
  273.0 52.2 %pool_backward.1 = (f32[256,4096]{1,0:T(8,128)}, f32[256,1024]{1,0:T(8,128)}, f32[256,256]{1,0:T(8,128)}, f32[256,64]{1,0:T(8,128)}) custom-call(f32[24,512]{1,0:T(8,128)} %get-tuple-element.26.ordered_ref.sorted_ref, bf16[6272,512]{1,0:T(8,128)(2,1)} %fusion.gp_ref), custom_call_target="tpu_custom_call" | custom-call | flops 40000000000 | bytes 10000000 | tf_op jit(solution)/shard_map/pool_backward/pallas_call | solution.py:232
  325.2 16.7 %collective-permute-start.4 = (f32[8,128]{1,0:T(8,128)S(1)}, f32[8,128]{1,0:T(8,128)S(1)}, u32[]{:S(2)}, u32[]{:S(2)}) collective-permute-start(f32[8,128]{1,0:T(8,128)S(1)} %add.129), channel_id=1, source_target_pairs={{0,16},{2,18},{4,20},{6,22},{8,24},{10,26},{12,28},{14,30},{16,0},... | collective-permute-start | bytes 12296 | tf_op jit(solution)/shard_map/ppermute | solution.py:460
  341.9 1.3 constant_dynamic-slice_fusion.3
  343.2 1.6 copy.59
  345.3 0.6 slice_bitcast_fusion.4
  346.3 1.5 collective-permute-start.21
  348.3 0.6 fusion.18
  349.0 0.6 slice_bitcast_fusion.3
  349.6 0.8 slice_bitcast_fusion
  350.3 21.3 %collective-permute-done.21 = bf16[512,1024]{1,0:T(8,128)(2,1)S(1)} collective-permute-done((bf16[512,1024]{1,0:T(8,128)(2,1)S(1)}, bf16[512,1024]{1,0:T(8,128)(2,1)S(1)}, u32[]{:S(2)}, u32[]{:S(2)}) %collective-permute-start.21) | collective-permute-done | bytes 1048608 | tf_op jit(solution)/shard_map/ppermute | solution.py:571
  371.8 2.4 maximum_convert_fusion
  374.2 14.5 %convert_element_type.229 = f32[6272,1024]{1,0:T(8,128)} convert(bf16[6272,1024]{1,0:T(8,128)(2,1)} %all-gather.2.cloned.1.call-done) | non-fusion elementwise | flops 6422528 | bytes 38535168 | tf_op jit(solution)/shard_map/convert_element_type | solution.py:565
  (94 shorter events, 5.4 us)
Async XLA Ops:
  7.2 367.1 %all-gather.2.cloned.1.call-start = ((), (), s32[]{:S(2)}) async-start(), calls=%async_computation | async-start | bytes 13647872 | tf_op jit(solution)/shard_map/all_gather | solution.py:565
  55.8 17.5 %copy-start = (bf16[6272,512]{1,0:T(8,128)(2,1)S(1)}, bf16[6272,512]{1,0:T(8,128)(2,1)}, u32[]{:S(2)}) copy-start(bf16[6272,512]{1,0:T(8,128)(2,1)} %get-tuple-element.27) | copy-start | bytes 19267588
  61.1 24.4 %copy-start.14 = (bf16[1024]{0:T(1024)(128)(2,1)S(1)}, bf16[1024]{0:T(1024)(128)(2,1)}, u32[]{:S(2)}) copy-start(bf16[1024]{0:T(1024)(128)(2,1)} %param.27) | copy-start | bytes 6148
  61.1 25.0 %copy-start.15 = (bf16[1024]{0:T(1024)(128)(2,1)S(1)}, bf16[1024]{0:T(1024)(128)(2,1)}, u32[]{:S(2)}) copy-start(bf16[1024]{0:T(1024)(128)(2,1)} %param.29) | copy-start | bytes 6148
  61.1 25.6 %copy-start.12 = (bf16[1024,4]{0,1:T(4,128)(2,1)S(1)}, bf16[1024,4]{0,1:T(4,128)(2,1)}, u32[]{:S(2)}) copy-start(bf16[1024,4]{0,1:T(4,128)(2,1)} %param.32) | copy-start | bytes 24580
  61.1 27.8 %copy-start.16 = (bf16[4]{0:T(256)(128)(2,1)S(1)}, bf16[4]{0:T(256)(128)(2,1)}, u32[]{:S(2)}) copy-start(bf16[4]{0:T(256)(128)(2,1)} %param.33) | copy-start | bytes 28
  61.1 27.8 %copy-start.17 = (bf16[81]{0:T(256)(128)(2,1)S(1)}, bf16[81]{0:T(256)(128)(2,1)}, u32[]{:S(2)}) copy-start(bf16[81]{0:T(256)(128)(2,1)} %param.31) | copy-start | bytes 490
  61.1 69.8 %collective-permute-start.5 = (bf16[8,392,512]{2,1,0:T(8,128)(2,1)}, bf16[8,392,512]{2,1,0:T(8,128)(2,1)}, u32[]{:S(2)}, u32[]{:S(2)}) collective-permute-start(bf16[8,392,512]{2,1,0:T(8,128)(2,1)} %get-tuple-element.83), channel_id=1, source_target_pairs={{0,2},{2,0},{4,6},{6,4},{8,10},{10,8},{12,14},{14,12},{16,18},{18,... | collective-permute-start | bytes 9633800 | tf_op jit(solution)/shard_map/ppermute | solution.py:528
  84.0 25.4 %collective-permute-start = (bf16[512,1024]{1,0:T(8,128)(2,1)}, bf16[512,1024]{1,0:T(8,128)(2,1)}, u32[]{:S(2)}, u32[]{:S(2)}) collective-permute-start(bf16[512,1024]{1,0:T(8,128)(2,1)} %convolution_convert_fusion.4.own_ref), channel_id=1, source_target_pairs={{0,1},{1,0},{2,3},{3,2},{4,5},{5,4},{6,7},{7,6},{8,9},{9,8},{10,11... | collective-permute-start | bytes 3145736 | tf_op jit(solution)/shard_map/ppermute | solution.py:522
  122.0 7.3 %collective-permute-start.6 = (bf16[512,1024]{1,0:T(8,128)(2,1)}, bf16[512,1024]{1,0:T(8,128)(2,1)}, u32[]{:S(2)}, u32[]{:S(2)}) collective-permute-start(bf16[512,1024]{1,0:T(8,128)(2,1)} %get-tuple-element.30), channel_id=1, source_target_pairs={{0,2},{2,0},{4,6},{6,4},{8,10},{10,8},{12,14},{14,12},{16,18},{18,... | collective-permute-start | bytes 3145736 | tf_op jit(solution)/shard_map/ppermute | solution.py:548
  123.4 1.1 copy-start.5
  125.4 2.6 collective-permute-start.13
  125.9 2.1 copy-start.6
  129.3 4.7 %copy-start.3 = (bf16[8,1,40,1024]{3,2,0,1:T(8,128)(2,1)}, bf16[8,1,40,1024]{3,2,0,1:T(8,128)(2,1)S(1)}, u32[]{:S(2)}) copy-start(bf16[8,1,40,1024]{3,2,0,1:T(8,128)(2,1)S(1)} %fusion.6) | copy-start | bytes 1966084
  134.0 1.1 copy-start.1
  136.3 28.0 %collective-permute-start.14 = (bf16[2,2,136,1024]{3,2,1,0:T(8,128)(2,1)}, bf16[2,2,136,1024]{3,2,1,0:T(8,128)(2,1)}, u32[]{:S(2)}, u32[]{:S(2)}) collective-permute-start(bf16[2,2,136,1024]{3,2,1,0:T(8,128)(2,1)} %fusion.10), channel_id=1, source_target_pairs={{0,8},{2,10},{4,12},{6,14},{8,0},{10,2},{12,4},{14,6},{16,24},{18,... | collective-permute-start | bytes 3342344 | tf_op jit(solution)/shard_map/ppermute | solution.py:451
  143.3 1.8 copy-start.9
  145.1 29.1 %collective-permute-start.7 = (bf16[4,1,144,1024]{3,2,0,1:T(8,128)(2,1)}, bf16[4,1,144,1024]{3,2,0,1:T(8,128)(2,1)}, u32[]{:S(2)}, u32[]{:S(2)}) collective-permute-start(bf16[4,1,144,1024]{3,2,0,1:T(8,128)(2,1)} %dynamic-slice_bitcast_fusion.3), channel_id=1, source_target_pairs={{0,4},{2,6},{4,0},{6,2},{8,12},{10,14},{12,8},{14,10},{16,20},{18,... | collective-permute-start | bytes 3538952 | tf_op jit(solution)/shard_map/ppermute | solution.py:451
  150.1 1.5 copy-start.7
  150.1 14.1 %copy-start.2 = (bf16[768,1024]{1,0:T(8,128)(2,1)S(1)}, bf16[768,1024]{1,0:T(8,128)(2,1)}, u32[]{:S(2)}) copy-start(bf16[768,1024]{1,0:T(8,128)(2,1)} %copy-done.1) | copy-start | bytes 4718596
  150.2 14.1 %copy-start.4 = (bf16[8,1,40,1024]{3,2,0,1:T(8,128)(2,1)S(1)}, bf16[8,1,40,1024]{3,2,0,1:T(8,128)(2,1)}, u32[]{:S(2)}) copy-start(bf16[8,1,40,1024]{3,2,0,1:T(8,128)(2,1)} %copy-done.3) | copy-start | bytes 1966084
  152.8 47.2 %collective-permute-start.10 = (bf16[4,1,152,1024]{3,2,0,1:T(8,128)(2,1)}, bf16[4,1,152,1024]{3,2,0,1:T(8,128)(2,1)S(1)}, u32[]{:S(2)}, u32[]{:S(2)}) collective-permute-start(bf16[4,1,152,1024]{3,2,0,1:T(8,128)(2,1)} %dynamic-slice_bitcast_fusion.2), channel_id=1, source_target_pairs={{0,4},{2,6},{4,0},{6,2},{8,12},{10,14},{12,8},{14,10},{16,20},{18,... | collective-permute-start | bytes 3735560 | tf_op jit(solution)/shard_map/ppermute | solution.py:451
  154.8 19.5 %copy-start.10 = (bf16[1152,1024]{1,0:T(8,128)(2,1)S(1)}, bf16[1152,1024]{1,0:T(8,128)(2,1)}, u32[]{:S(2)}) copy-start(bf16[1152,1024]{1,0:T(8,128)(2,1)} %copy-done.9) | copy-start | bytes 7077892
  166.0 34.0 %copy-start.8 = (bf16[1216,1024]{1,0:T(8,128)(2,1)S(1)}, bf16[1216,1024]{1,0:T(8,128)(2,1)}, u32[]{:S(2)}) copy-start(bf16[1216,1024]{1,0:T(8,128)(2,1)} %copy-done.7) | copy-start | bytes 7471108
  166.0 34.9 %collective-permute-start.15 = (bf16[1,2,136,1024]{3,2,1,0:T(8,128)(2,1)S(1)}, bf16[1,2,136,1024]{3,2,1,0:T(8,128)(2,1)S(1)}, u32[]{:S(2)}, u32[]{:S(2)}) collective-permute-start(bf16[1,2,136,1024]{3,2,1,0:T(8,128)(2,1)S(1)} %constant_dynamic-slice_fusion), channel_id=1, source_target_pairs={{0,16},{2,18},{4,20},{6,22},{8,24},{10,26},{12,28},{14,30},{16,0},... | collective-permute-start | bytes 1671176 | tf_op jit(solution)/shard_map/ppermute | solution.py:451
  176.1 25.4 %collective-permute-start.8 = (bf16[2,144,1024]{2,1,0:T(8,128)(2,1)S(1)}, bf16[2,144,1024]{2,1,0:T(8,128)(2,1)S(1)}, u32[]{:S(2)}, u32[]{:S(2)}) collective-permute-start(bf16[2,144,1024]{2,1,0:T(8,128)(2,1)S(1)} %dynamic-slice_bitcast_fusion.6), channel_id=1, source_target_pairs={{0,8},{2,10},{4,12},{6,14},{8,0},{10,2},{12,4},{14,6},{16,24},{18,... | collective-permute-start | bytes 1769480 | tf_op jit(solution)/shard_map/ppermute | solution.py:451
  200.5 21.6 %collective-permute-start.11 = (bf16[2,152,1024]{2,1,0:T(8,128)(2,1)S(1)}, bf16[2,152,1024]{2,1,0:T(8,128)(2,1)S(1)}, u32[]{:S(2)}, u32[]{:S(2)}) collective-permute-start(bf16[2,152,1024]{2,1,0:T(8,128)(2,1)S(1)} %dynamic-slice_bitcast_fusion.5), channel_id=1, source_target_pairs={{0,8},{2,10},{4,12},{6,14},{8,0},{10,2},{12,4},{14,6},{16,24},{18,... | collective-permute-start | bytes 1867784 | tf_op jit(solution)/shard_map/ppermute | solution.py:451
  201.1 21.9 %collective-permute-start.16 = (bf16[1,136,1024]{2,1,0:T(8,128)(2,1)S(1)}, bf16[1,136,1024]{2,1,0:T(8,128)(2,1)S(1)}, u32[]{:S(2)}, u32[]{:S(2)}) collective-permute-start(bf16[1,136,1024]{2,1,0:T(8,128)(2,1)S(1)} %dynamic-slice_bitcast_fusion.7), channel_id=1, source_target_pairs={{0,4},{2,6},{4,0},{6,2},{8,12},{10,14},{12,8},{14,10},{16,20},{18,... | collective-permute-start | bytes 835592 | tf_op jit(solution)/shard_map/ppermute | solution.py:451
  201.8 21.3 %collective-permute-start.9 = (bf16[1,144,1024]{2,1,0:T(8,128)(2,1)S(1)}, bf16[1,144,1024]{2,1,0:T(8,128)(2,1)S(1)}, u32[]{:S(2)}, u32[]{:S(2)}) collective-permute-start(bf16[1,144,1024]{2,1,0:T(8,128)(2,1)S(1)} %constant_dynamic-slice_fusion.2), channel_id=1, source_target_pairs={{0,16},{2,18},{4,20},{6,22},{8,24},{10,26},{12,28},{14,30},{16,0},... | collective-permute-start | bytes 884744 | tf_op jit(solution)/shard_map/ppermute | solution.py:451
  222.4 15.0 %collective-permute-start.12 = (bf16[1,152,1024]{2,1,0:T(8,128)(2,1)S(1)}, bf16[1,152,1024]{2,1,0:T(8,128)(2,1)S(1)}, u32[]{:S(2)}, u32[]{:S(2)}) collective-permute-start(bf16[1,152,1024]{2,1,0:T(8,128)(2,1)S(1)} %constant_dynamic-slice_fusion.1), channel_id=1, source_target_pairs={{0,16},{2,18},{4,20},{6,22},{8,24},{10,26},{12,28},{14,30},{16,0},... | collective-permute-start | bytes 933896 | tf_op jit(solution)/shard_map/ppermute | solution.py:451
  223.2 21.5 %copy-start.13 = (f32[8,128]{1,0:T(8,128)S(1)}, f32[8,128]{1,0:T(8,128)}, u32[]{:S(2)}) copy-start(f32[8,128]{1,0:T(8,128)} %get-tuple-element.28) | copy-start | bytes 12292
  237.5 21.8 %copy-start.11 = (bf16[512,1024]{1,0:T(8,128)(2,1)S(1)}, bf16[512,1024]{1,0:T(8,128)(2,1)}, u32[]{:S(2)}) copy-start(bf16[512,1024]{1,0:T(8,128)(2,1)} %get-tuple-element.30) | copy-start | bytes 3145732
  238.5 6.1 %collective-permute-start.17 = (bf16[40,1024]{1,0:T(8,128)(2,1)S(1)}, bf16[40,1024]{1,0:T(8,128)(2,1)S(1)}, u32[]{:S(2)}, u32[]{:S(2)}) collective-permute-start(bf16[40,1024]{1,0:T(8,128)(2,1)S(1)} %slice_bitcast_fusion.2), channel_id=1, source_target_pairs={{0,16},{2,18},{4,20},{6,22},{8,24},{10,26},{12,28},{14,30},{16,0},... | collective-permute-start | bytes 245768 | tf_op jit(solution)/shard_map/ppermute | solution.py:477
  244.6 11.8 %collective-permute-start.18 = (bf16[2,40,1024]{2,1,0:T(8,128)(2,1)S(1)}, bf16[2,40,1024]{2,1,0:T(8,128)(2,1)S(1)}, u32[]{:S(2)}, u32[]{:S(2)}) collective-permute-start(bf16[2,40,1024]{2,1,0:T(8,128)(2,1)S(1)} %pad_maximum_fusion.6), channel_id=1, source_target_pairs={{0,8},{2,10},{4,12},{6,14},{8,0},{10,2},{12,4},{14,6},{16,24},{18,... | collective-permute-start | bytes 491528 | tf_op jit(solution)/shard_map/ppermute | solution.py:477
  244.7 1.2 collective-permute-start.1
  245.9 26.8 %collective-permute-start.2 = (f32[8,128]{1,0:T(8,128)S(1)}, f32[8,128]{1,0:T(8,128)S(1)}, u32[]{:S(2)}, u32[]{:S(2)}) collective-permute-start(f32[8,128]{1,0:T(8,128)S(1)} %add.127), channel_id=1, source_target_pairs={{0,4},{2,6},{4,0},{6,2},{8,12},{10,14},{12,8},{14,10},{16,20},{18,... | collective-permute-start | bytes 12296 | tf_op jit(solution)/shard_map/ppermute | solution.py:460
  256.4 16.3 %collective-permute-start.19 = (bf16[2,2,40,1024]{3,2,0,1:T(8,128)(2,1)S(1)}, bf16[2,2,40,1024]{3,2,0,1:T(8,128)(2,1)S(1)}, u32[]{:S(2)}, u32[]{:S(2)}) collective-permute-start(bf16[2,2,40,1024]{3,2,0,1:T(8,128)(2,1)S(1)} %pad_maximum_fusion.5), channel_id=1, source_target_pairs={{0,4},{2,6},{4,0},{6,2},{8,12},{10,14},{12,8},{14,10},{16,20},{18,... | collective-permute-start | bytes 983048 | tf_op jit(solution)/shard_map/ppermute | solution.py:477
  272.8 52.4 %collective-permute-start.3 = (f32[8,128]{1,0:T(8,128)S(1)}, f32[8,128]{1,0:T(8,128)S(1)}, u32[]{:S(2)}, u32[]{:S(2)}) collective-permute-start(f32[8,128]{1,0:T(8,128)S(1)} %add.128), channel_id=1, source_target_pairs={{0,8},{2,10},{4,12},{6,14},{8,0},{10,2},{12,4},{14,6},{16,24},{18,... | collective-permute-start | bytes 12296 | tf_op jit(solution)/shard_map/ppermute | solution.py:460
  272.9 73.0 %collective-permute-start.20 = (bf16[2,2,2,40,1024]{4,3,0,1,2:T(8,128)(2,1)S(1)}, bf16[2,2,2,40,1024]{4,3,0,1,2:T(8,128)(2,1)S(1)}, u32[]{:S(2)}, u32[]{:S(2)}) collective-permute-start(bf16[2,2,2,40,1024]{4,3,0,1,2:T(8,128)(2,1)S(1)} %pad_maximum_fusion.4), channel_id=1, source_target_pairs={{0,2},{2,0},{4,6},{6,4},{8,10},{10,8},{12,14},{14,12},{16,18},{18,... | collective-permute-start | bytes 1966088 | tf_op jit(solution)/shard_map/ppermute | solution.py:477
  325.2 19.6 %collective-permute-start.4 = (f32[8,128]{1,0:T(8,128)S(1)}, f32[8,128]{1,0:T(8,128)S(1)}, u32[]{:S(2)}, u32[]{:S(2)}) collective-permute-start(f32[8,128]{1,0:T(8,128)S(1)} %add.129), channel_id=1, source_target_pairs={{0,16},{2,18},{4,20},{6,22},{8,24},{10,26},{12,28},{14,30},{16,0},... | collective-permute-start | bytes 12296 | tf_op jit(solution)/shard_map/ppermute | solution.py:460
  346.3 25.3 %collective-permute-start.21 = (bf16[512,1024]{1,0:T(8,128)(2,1)S(1)}, bf16[512,1024]{1,0:T(8,128)(2,1)S(1)}, u32[]{:S(2)}, u32[]{:S(2)}) collective-permute-start(bf16[512,1024]{1,0:T(8,128)(2,1)S(1)} %slice.76), channel_id=1, source_target_pairs={{0,1},{1,0},{2,3},{3,2},{4,5},{5,4},{6,7},{7,6},{8,9},{9,8},{10,11... | collective-permute-start | bytes 3145736 | tf_op jit(solution)/shard_map/ppermute | solution.py:571
Sparse Core Ops, SparseCore 0:
  238.6 102.2 all-gather.1
